TPU v7x, 32 devices: a whole 2x2x4 slice. The times are simulated.
32 devices in a mesh: dp: 2 (over y), fsdp: 16 (over z, x, core).
Axes of the slice: x: 2, y: 2, z: 4, core: 2. Of those that a mesh axis runs over, the one named last changes fastest.
Arguments:
- tokens: bfloat16 [16384, 768], P(('dp', 'fsdp')), may hold values from -6 to 6
- lengths: int32 [32], P(('dp', 'fsdp')), may hold values from 256 to 500, as said below
- buckets: int32 [32, 512, 512], P(('dp', 'fsdp')), may hold values from 0 to 447, as said below
- ln1_gain: bfloat16 [768], P(('dp', 'fsdp')), may hold values from 0.5 to 1.5
- ln1_bias: bfloat16 [768], P(('dp', 'fsdp')), may hold values from -3 to 3
- qkv_weight: bfloat16 [768, 2304], P(('dp', 'fsdp')), may hold values from -0.21875 to 0.21875
- q_bias: bfloat16 [768], P(('dp', 'fsdp')), may hold values from -3 to 3
- v_bias: bfloat16 [768], P(('dp', 'fsdp')), may hold values from -3 to 3
- out_weight: bfloat16 [768, 768], P(('dp', 'fsdp')), may hold values from -0.875 to 0.875
- out_bias: bfloat16 [768], P(('dp', 'fsdp')), may hold values from -3 to 3
- rel_table: bfloat16 [12, 448], replicated, may hold values from -4 to 4
- ln2_gain: bfloat16 [768], P(('dp', 'fsdp')), may hold values from 0.5 to 1.5
- ln2_bias: bfloat16 [768], P(('dp', 'fsdp')), may hold values from -3 to 3
- up_weight: bfloat16 [768, 3072], P(('dp', 'fsdp')), may hold values from -0.21875 to 0.21875
- up_bias: bfloat16 [3072], P(('dp', 'fsdp')), may hold values from -3 to 3
- down_weight: bfloat16 [3072, 768], P(('dp', 'fsdp')), may hold values from -0.109375 to 0.109375
- down_bias: bfloat16 [768], P(('dp', 'fsdp')), may hold values from -3 to 3
- cotangent: bfloat16 [16384, 768], P(('dp', 'fsdp')), may hold values from -6 to 6
Outputs:
- output: bfloat16 [16384, 768], P(('dp', 'fsdp'))
- input_grad: float32 [16384, 768], P(('dp', 'fsdp'))
- grad_ln1_gain: float32 [768], P(('dp', 'fsdp'))
- grad_ln1_bias: float32 [768], P(('dp', 'fsdp'))
- grad_qkv_weight: float32 [768, 2304], P(('dp', 'fsdp'))
- grad_q_bias: float32 [768], P(('dp', 'fsdp'))
- grad_v_bias: float32 [768], P(('dp', 'fsdp'))
- grad_out_weight: float32 [768, 768], P(('dp', 'fsdp'))
- grad_out_bias: float32 [768], P(('dp', 'fsdp'))
- grad_rel_table: float32 [12, 448], replicated
- grad_ln2_gain: float32 [768], P(('dp', 'fsdp'))
- grad_ln2_bias: float32 [768], P(('dp', 'fsdp'))
- grad_up_weight: float32 [768, 3072], P(('dp', 'fsdp'))
- grad_up_bias: float32 [3072], P(('dp', 'fsdp'))
- grad_down_weight: float32 [3072, 768], P(('dp', 'fsdp'))
- grad_down_bias: float32 [768], P(('dp', 'fsdp'))
Inputs may be any that keep to these rules, and one draw needn't show every extreme that they name: `lengths`: each item is speech, with 380 to 500 live rows, or text, with exactly 256; item 0 is speech with 500 rows and item 1 is text. With t = j - i: for a speech item buckets[n, i, j] = clip(t, -160, 159) + 160; for a text item 2 * 160 + clip(t, -64, 63) + 64.
All inputs are finite; a program needn't handle non-finite values.
Results may differ from a plain program's by a relative error of at most 0.014.
Values may be sent and summed in bfloat16 or wider, within the bound.
No kernel may reach another device: no remote copies, remote signals or barrier semaphores. Data moves between devices by JAX's collectives and lax.ppermute only.
A program may use at most 320 MiB of HBM per device.

v0:
```python
import jax
import jax.numpy as jnp
from jax import lax
from jax.sharding import PartitionSpec as P


def normalize(row_data, gain_vec, bias_vec):
    centre = row_data - jnp.mean(row_data, -1, keepdims=True)
    spread = jnp.mean(centre * centre, -1, keepdims=True)
    return centre * lax.rsqrt(spread + 1e-05) * gain_vec + bias_vec


def gelu_exact(argument):
    return 0.5 * argument * (1.0 + lax.erf(argument * 0.7071067811865476))


def contract_rows(left_side, right_side):
    return lax.dot_general(
        left_side, right_side, (((0,), (0,)), ((), ())), preferred_element_type=jnp.float32
    )


def contract_cols(left_side, right_side):
    return lax.dot_general(
        left_side, right_side, (((1,), (1,)), ((), ())), preferred_element_type=jnp.float32
    )


def table_gradient(grad_scores, bucket, number):
    head_count, slot_len, unused = grad_scores.shape
    block_rows = min(64, slot_len)
    block_count = slot_len // block_rows
    labels = jnp.arange(number, dtype=jnp.int32)
    score_blocks = grad_scores.reshape(head_count, block_count, block_rows * slot_len).transpose(
        1, 0, 2
    )
    bucket_blocks = bucket.reshape(block_count, block_rows * slot_len)

    def one_block(total, packed):
        score_block, bucket_block = packed
        indicator = (bucket_block[:, None] == labels[None, :]).astype(jnp.bfloat16)
        return (total + jnp.dot(score_block, indicator, preferred_element_type=jnp.float32), None)

    total, unused_out = lax.scan(
        one_block, jnp.zeros((head_count, number), jnp.float32), (score_blocks, bucket_blocks)
    )
    return total


def on_device(
    tokens,
    lengths,
    buckets,
    ln1_gain,
    ln1_bias,
    qkv_weight,
    q_bias,
    v_bias,
    out_weight,
    out_bias,
    rel_table,
    ln2_gain,
    ln2_bias,
    up_weight,
    up_bias,
    down_weight,
    down_bias,
    cotangent,
):
    members = lengths.shape[0]
    slot_len = buckets.shape[1]
    model_width = tokens.shape[1]
    head_count = rel_table.shape[0]
    number = rel_table.shape[1]
    head_size = model_width // head_count
    score_scale = head_size ** (-0.5)
    table_float = rel_table.astype(jnp.float32)
    places = jnp.arange(slot_len, dtype=jnp.int32)
    live_mask = places[None, :] < lengths[:, None]
    live_rows = live_mask.reshape(-1)[:, None]
    gain_first, bias_first, w_qkv, bias_q, bias_v, w_out, bias_out = (
        lax.all_gather(ln1_gain, ("dp", "fsdp"), axis=0, tiled=True),
        lax.all_gather(ln1_bias, ("dp", "fsdp"), axis=0, tiled=True),
        lax.all_gather(qkv_weight, ("dp", "fsdp"), axis=0, tiled=True),
        lax.all_gather(q_bias, ("dp", "fsdp"), axis=0, tiled=True),
        lax.all_gather(v_bias, ("dp", "fsdp"), axis=0, tiled=True),
        lax.all_gather(out_weight, ("dp", "fsdp"), axis=0, tiled=True),
        lax.all_gather(out_bias, ("dp", "fsdp"), axis=0, tiled=True),
    )
    inputs = tokens.astype(jnp.float32)
    normed_f, norm_first_back = jax.vjp(
        normalize, inputs, gain_first.astype(jnp.float32), bias_first.astype(jnp.float32)
    )
    normed = normed_f.astype(jnp.bfloat16)
    qkv_bias = jnp.concatenate(
        [
            bias_q.astype(jnp.float32),
            jnp.zeros((model_width,), jnp.float32),
            bias_v.astype(jnp.float32),
        ]
    )
    joined = (jnp.dot(normed, w_qkv, preferred_element_type=jnp.float32) + qkv_bias).astype(
        jnp.bfloat16
    )
    split_heads = joined.reshape(members, slot_len, 3, head_count, head_size)
    queries = split_heads[:, :, 0]
    key_rows = split_heads[:, :, 1]
    values = split_heads[:, :, 2]

    def forward_item(packed):
        q_item, k_item, v_item, bucket, allowed = packed
        scores = (
            jnp.einsum("qhd,khd->hqk", q_item, k_item, preferred_element_type=jnp.float32)
            * score_scale
            + table_float[:, bucket]
        )
        scores = jnp.where(allowed[None, None, :], scores, -1e30)
        peak_score = jnp.max(scores, -1, keepdims=True)
        raised = jnp.exp(scores - peak_score)
        total_sum = jnp.sum(raised, -1, keepdims=True)
        probs_low = (raised / total_sum).astype(jnp.bfloat16)
        mixed = jnp.einsum("hqk,khd->qhd", probs_low, v_item, preferred_element_type=jnp.float32)
        return (mixed.astype(jnp.bfloat16).reshape(slot_len, model_width), peak_score, total_sum)

    mixed_all, peaks, sums_all = lax.map(
        forward_item, (queries, key_rows, values, buckets, live_mask)
    )
    mixed_rows = mixed_all.reshape(members * slot_len, model_width)
    branch = jnp.dot(mixed_rows, w_out, preferred_element_type=jnp.float32) + bias_out.astype(
        jnp.float32
    )
    residual = inputs + branch
    gain_second, bias_second, w_up, bias_up, w_down, bias_down = (
        lax.all_gather(ln2_gain, ("dp", "fsdp"), axis=0, tiled=True),
        lax.all_gather(ln2_bias, ("dp", "fsdp"), axis=0, tiled=True),
        lax.all_gather(up_weight, ("dp", "fsdp"), axis=0, tiled=True),
        lax.all_gather(up_bias, ("dp", "fsdp"), axis=0, tiled=True),
        lax.all_gather(down_weight, ("dp", "fsdp"), axis=0, tiled=True),
        lax.all_gather(down_bias, ("dp", "fsdp"), axis=0, tiled=True),
    )
    normed_two_f, norm_second_back = jax.vjp(
        normalize, residual, gain_second.astype(jnp.float32), bias_second.astype(jnp.float32)
    )
    normed_two = normed_two_f.astype(jnp.bfloat16)
    pre_act = jnp.dot(normed_two, w_up, preferred_element_type=jnp.float32) + bias_up.astype(
        jnp.float32
    )
    active_f, gelu_back = jax.vjp(gelu_exact, pre_act)
    active = active_f.astype(jnp.bfloat16)
    result = (
        residual
        + jnp.dot(active, w_down, preferred_element_type=jnp.float32)
        + bias_down.astype(jnp.float32)
    )
    output = jnp.where(live_rows, result, 0.0).astype(jnp.bfloat16)
    grad_result = jnp.where(live_rows, cotangent, jnp.zeros_like(cotangent))
    w_up_back, w_down_back = (
        lax.all_gather(up_weight, ("dp", "fsdp"), axis=0, tiled=True),
        lax.all_gather(down_weight, ("dp", "fsdp"), axis=0, tiled=True),
    )
    grad_down = contract_rows(active, grad_result)
    grad_down_bias = jnp.sum(grad_result, 0, dtype=jnp.float32)
    grad_active = contract_cols(grad_result, w_down_back)
    (grad_pre,) = gelu_back(grad_active)
    grad_pre_low = grad_pre.astype(jnp.bfloat16)
    grad_up = contract_rows(normed_two, grad_pre_low)
    grad_up_bias = jnp.sum(grad_pre_low, 0, dtype=jnp.float32)
    grad_normed_two = contract_cols(grad_pre_low, w_up_back)
    grad_resid_norm, grad_gain_second, grad_bias_second = norm_second_back(grad_normed_two)
    grad_residual = grad_result.astype(jnp.float32) + grad_resid_norm
    ffn_parts = (
        lax.psum_scatter(grad_gain_second, ("dp", "fsdp"), scatter_dimension=0, tiled=True),
        lax.psum_scatter(grad_bias_second, ("dp", "fsdp"), scatter_dimension=0, tiled=True),
        lax.psum_scatter(grad_up, ("dp", "fsdp"), scatter_dimension=0, tiled=True),
        lax.psum_scatter(grad_up_bias, ("dp", "fsdp"), scatter_dimension=0, tiled=True),
        lax.psum_scatter(grad_down, ("dp", "fsdp"), scatter_dimension=0, tiled=True),
        lax.psum_scatter(grad_down_bias, ("dp", "fsdp"), scatter_dimension=0, tiled=True),
    )
    w_qkv_back, w_out_back = (
        lax.all_gather(qkv_weight, ("dp", "fsdp"), axis=0, tiled=True),
        lax.all_gather(out_weight, ("dp", "fsdp"), axis=0, tiled=True),
    )
    grad_branch = grad_residual.astype(jnp.bfloat16)
    grad_out_w = contract_rows(mixed_rows, grad_branch)
    grad_out_b = jnp.sum(grad_branch, 0, dtype=jnp.float32)
    grad_mixed = (
        contract_cols(grad_branch, w_out_back)
        .astype(jnp.bfloat16)
        .reshape(members, slot_len, head_count, head_size)
    )

    def backward_item(packed):
        q_item, k_item, v_item, grad_item, bucket, allowed, peak_score, total_sum = packed
        scores = (
            jnp.einsum("qhd,khd->hqk", q_item, k_item, preferred_element_type=jnp.float32)
            * score_scale
            + table_float[:, bucket]
        )
        scores = jnp.where(allowed[None, None, :], scores, -1e30)
        probs = jnp.exp(scores - peak_score) / total_sum
        probs_low = probs.astype(jnp.bfloat16)
        grad_v = jnp.einsum(
            "hqk,qhd->khd", probs_low, grad_item, preferred_element_type=jnp.float32
        )
        grad_probs = jnp.einsum(
            "qhd,khd->hqk", grad_item, v_item, preferred_element_type=jnp.float32
        )
        grad_scores = (
            probs * (grad_probs - jnp.sum(probs * grad_probs, -1, keepdims=True))
        ).astype(jnp.bfloat16)
        grad_q = (
            jnp.einsum("hqk,khd->qhd", grad_scores, k_item, preferred_element_type=jnp.float32)
            * score_scale
        )
        grad_k = (
            jnp.einsum("hqk,qhd->khd", grad_scores, q_item, preferred_element_type=jnp.float32)
            * score_scale
        )
        stacked = (
            jnp.stack([grad_q, grad_k, grad_v], 1)
            .astype(jnp.bfloat16)
            .reshape(slot_len, 3 * model_width)
        )
        table_term = table_gradient(grad_scores, bucket, number)
        return (stacked, table_term)

    grad_joined, table_parts = lax.map(
        backward_item, (queries, key_rows, values, grad_mixed, buckets, live_mask, peaks, sums_all)
    )
    grad_joined = grad_joined.reshape(members * slot_len, 3 * model_width)
    grad_qkv = contract_rows(normed, grad_joined)
    column_sums = jnp.sum(grad_joined, 0, dtype=jnp.float32)
    grad_bias_q = column_sums[:model_width]
    grad_bias_v = column_sums[2 * model_width :]
    grad_normed = contract_cols(grad_joined, w_qkv_back)
    grad_inputs_norm, grad_gain_first, grad_bias_first = norm_first_back(grad_normed)
    input_grad = grad_residual + grad_inputs_norm
    attn_parts = (
        lax.psum_scatter(grad_gain_first, ("dp", "fsdp"), scatter_dimension=0, tiled=True),
        lax.psum_scatter(grad_bias_first, ("dp", "fsdp"), scatter_dimension=0, tiled=True),
        lax.psum_scatter(grad_qkv, ("dp", "fsdp"), scatter_dimension=0, tiled=True),
        lax.psum_scatter(grad_bias_q, ("dp", "fsdp"), scatter_dimension=0, tiled=True),
        lax.psum_scatter(grad_bias_v, ("dp", "fsdp"), scatter_dimension=0, tiled=True),
        lax.psum_scatter(grad_out_w, ("dp", "fsdp"), scatter_dimension=0, tiled=True),
        lax.psum_scatter(grad_out_b, ("dp", "fsdp"), scatter_dimension=0, tiled=True),
    )
    grad_table = lax.psum(jnp.sum(table_parts, 0), ("dp", "fsdp"))
    return (
        output,
        input_grad,
        attn_parts[0],
        attn_parts[1],
        attn_parts[2],
        attn_parts[3],
        attn_parts[4],
        attn_parts[5],
        attn_parts[6],
        grad_table,
        ffn_parts[0],
        ffn_parts[1],
        ffn_parts[2],
        ffn_parts[3],
        ffn_parts[4],
        ffn_parts[5],
    )


def solution(mesh):
    in_specs = (
        P(("dp", "fsdp"), None),
        P(("dp", "fsdp")),
        P(("dp", "fsdp"), None, None),
        P(("dp", "fsdp")),
        P(("dp", "fsdp")),
        P(("dp", "fsdp"), None),
        P(("dp", "fsdp")),
        P(("dp", "fsdp")),
        P(("dp", "fsdp"), None),
        P(("dp", "fsdp")),
        P(),
        P(("dp", "fsdp")),
        P(("dp", "fsdp")),
        P(("dp", "fsdp"), None),
        P(("dp", "fsdp")),
        P(("dp", "fsdp"), None),
        P(("dp", "fsdp")),
        P(("dp", "fsdp"), None),
    )
    out_specs = (
        P(("dp", "fsdp"), None),
        P(("dp", "fsdp"), None),
        P(("dp", "fsdp")),
        P(("dp", "fsdp")),
        P(("dp", "fsdp"), None),
        P(("dp", "fsdp")),
        P(("dp", "fsdp")),
        P(("dp", "fsdp"), None),
        P(("dp", "fsdp")),
        P(),
        P(("dp", "fsdp")),
        P(("dp", "fsdp")),
        P(("dp", "fsdp"), None),
        P(("dp", "fsdp")),
        P(("dp", "fsdp"), None),
        P(("dp", "fsdp")),
    )
    return jax.shard_map(
        on_device, mesh=mesh, in_specs=in_specs, out_specs=out_specs, check_vma=False
    )
```

profile of v0, /device:TPU:0, one launch (start us, length us, event | category | flops | bytes accessed | tf_op | source)
XLA Modules:
  0.0 1585.9 jit_solution(18067826354804290504)
XLA Ops:
  17.6 42.8 %all-reduce.19 = (bf16[768]{0:T(1024)(128)(2,1)S(1)}, bf16[768]{0:T(1024)(128)(2,1)S(1)}, bf16[768]{0:T(1024)(128)(2,1)S(1)}, bf16[768]{0:T(1024)(128)(2,1)S(1)}...) all-reduce(bf16[768]{0:T(1024)(128)(2,1)S(1)} %dynamic-update-slice, ...), channel_id=1, replica_groups=mesh['dp'=2,'fsdp'=16] {'dp','fsdp'}, use_global_device_ids=true, to_apply=%add.3 | all-reduce | flops 9216 | bytes 36864
  63.0 860.0 %gather_fusion = f32[262144,12]{1,0:T(8,128)} fusion(f32[12,448]{0,1:T(8,128)S(1)} %copy.67, s32[262144]{0:T(1024)S(1)} %broadcast_clamp_fusion), kind=kCustom, calls=%fused_computation | custom fusion | bytes 26214400 | tf_op jit(solution)/shard_map/while/body/eval_jaxpr/gather | solution.py:115
  923.0 73.5 %copy.69 = f32[512,512,12]{0,1,2:T(8,128)} copy(f32[512,512,12]{2,1,0:T(8,128)} %bitcast.6) | data formatting | bytes 25165824 | tf_op jit(solution)/shard_map/while/body/eval_jaxpr/gather | solution.py:115
  1005.6 9.0 fusion.9
  1014.6 15.2 fusion.49
  1029.8 12.1 fusion.29
  1045.8 8.4 multiply_convert_fusion.1
  1076.4 12.6 fusion.26
  1089.1 10.8 multiply_reduce_fusion
  1132.0 9.2 copy.75
  1141.2 10.5 reshape.192
  1151.6 10.0 copy.76
  1166.8 104.2 %while.14 = (s32[]{:T(128)}, f32[12,448]{1,0:T(8,128)S(1)}, bf16[8,12,32768]{2,1,0:T(8,128)(2,1)}, s32[8,32768]{1,0:T(8,128)}, s32[]{:T(128)}, /*index=5*/s32[]{:T(128)}) while((s32[]{:T(128)}, f32[12,448]{1,0:T(8,128)S(1)}, bf16[8,12,32768]{2,1,0:T(8,128)(2,1)}, s32[8,32768]{1,0:T(8,128)}, s32[]{:T(128)}, ...), condition=%wide.region_23.24_spmd.clone, body=%wide.region_22.23_spmd.clone.sunk | while | flops 367012352 | bytes 1485395 | solution.py:44
  1168.4 11.6 fusion.80
  1181.3 11.6 fusion.80
  1194.3 11.7 fusion.80
  1207.3 11.6 fusion.80
  1220.3 11.6 fusion.80
  1233.2 11.6 fusion.80
  1246.2 11.6 fusion.80
  1259.2 11.7 fusion.80
  1279.8 42.2 %all-reduce.18 = (f32[768]{0:T(1024)S(1)}, f32[768]{0:T(1024)S(1)}, f32[768]{0:T(1024)S(1)}, f32[768]{0:T(1024)S(1)}, f32[768]{0:T(1024)S(1)}, /*index=5*/f32[12...) all-reduce(f32[768]{0:T(1024)S(1)} %get-tuple-element.141, ...), channel_id=2, replica_groups=mesh['dp'=2,'fsdp'=16] {'dp','fsdp'}, use_global_device_ids=true, to_apply=%region_12.13.clone | all-reduce | flops 14592 | bytes 116736
  1334.4 102.4 %reduce-scatter.9.cloned.1.call-done = f32[24,3072]{1,0:T(8,128)} async-done(((f32[768,3072]{1,0:T(8,128)}), f32[24,3072]{1,0:T(8,128)}) %reduce-scatter.9.cloned.1.call-update) | async-done | bytes 294928 | tf_op jit(solution)/shard_map/reduce_scatter | solution.py:174
  1436.9 142.0 %reduce-scatter.11.cloned.1.call-done = f32[96,768]{1,0:T(8,128)} async-done(((f32[3072,768]{1,0:T(8,128)}), f32[96,768]{1,0:T(8,128)}) %reduce-scatter.11.cloned.1.call-update) | async-done | bytes 294928 | tf_op jit(solution)/shard_map/reduce_scatter | solution.py:176
  (159 shorter events, 116.2 us)
Async XLA Ops:
  7.2 55.6 %copy-start.16 = (bf16[12,448]{1,0:T(8,128)(2,1)S(1)}, bf16[12,448]{1,0:T(8,128)(2,1)}, u32[]{:S(2)}) copy-start(bf16[12,448]{1,0:T(8,128)(2,1)} %param.30) | copy-start | bytes 32260
  7.2 990.0 %all-gather.5.cloned.1.call-start = ((), (), s32[]{:S(2)}) async-start(), calls=%async_computation.4 | async-start | bytes 3649536 | tf_op jit(solution)/shard_map/all_gather | solution.py:84
  7.9 1034.0 %all-gather.7.cloned.1.call-start = ((), (), s32[]{:S(2)}) async-start(), calls=%async_computation.5 | async-start | bytes 1216512 | tf_op jit(solution)/shard_map/all_gather | solution.py:87
  8.7 1037.1 %all-gather.9.cloned.1.call-start = ((), (), s32[]{:S(2)}) async-start(), calls=%async_computation.6 | async-start | bytes 4866048 | tf_op jit(solution)/shard_map/all_gather | solution.py:136
  9.4 1044.9 %all-gather.11.cloned.1.call-start = ((), (), s32[]{:S(2)}) async-start(), calls=%async_computation.7 | async-start | bytes 4866048 | tf_op jit(solution)/shard_map/all_gather | solution.py:138
  10.0 1324.4 %reduce-scatter.7.cloned.1.call-start = ((), (), s32[]{:S(2)}) async-start(), calls=%async_computation.9 | async-start | bytes 2433024 | tf_op jit(solution)/shard_map/reduce_scatter | solution.py:244
  923.0 73.6 %copy-start.3 = (bf16[512,768]{1,0:T(8,128)(2,1)S(1)}, bf16[512,768]{1,0:T(8,128)(2,1)}, u32[]{:S(2)}) copy-start(bf16[512,768]{1,0:T(8,128)(2,1)} %param.20) | copy-start | bytes 2359300
  997.2 5.6 copy-start.14
  1054.3 8.3 copy-start.5
  1054.3 8.3 copy-start.18
  1062.5 3.0 copy-start.20
  1066.2 2.4 copy-start.13
  1070.9 263.5 %reduce-scatter.5.cloned.1.call-start = ((), (), s32[]{:S(2)}) async-start(), calls=%async_computation.8 | async-start | bytes 7299072 | tf_op jit(solution)/shard_map/reduce_scatter | solution.py:241
  1089.1 10.8 slice-start
  1089.1 11.9 slice-start.1
  1089.1 13.2 slice-start.2
  1109.2 2.7 copy-start
  1111.9 2.0 copy-start.12
  1121.0 315.9 %reduce-scatter.9.cloned.1.call-start = ((), (), s32[]{:S(2)}) async-start(), calls=%async_computation.10 | async-start | bytes 9732096 | tf_op jit(solution)/shard_map/reduce_scatter | solution.py:174
  1129.5 2.5 copy-start.17
  1129.5 449.3 %reduce-scatter.11.cloned.1.call-start = ((), (), s32[]{:S(2)}) async-start(), calls=%async_computation.11 | async-start | bytes 9732096 | tf_op jit(solution)/shard_map/reduce_scatter | solution.py:176
  1151.6 10.0 copy-start.8
  1151.6 10.0 copy-start.19
  1271.2 5.1 copy-start.15
  (8 other events, 10.9 us)
Sparse Core Ops, SparseCore 0:
  10.9 62.8 all-gather.4
  76.7 52.8 all-gather.6
  132.5 62.5 all-gather.8
  197.8 62.3 all-gather.10
  1071.0 99.1 reduce-scatter.6
  1177.3 118.1 reduce-scatter.4
  1302.0 134.8 reduce-scatter.8
  1444.3 134.4 reduce-scatter.10
where the time goes:
time: 1600 us; the launch traced here: 1590 us
  local copies, waits for them, and re-layouts  1010 us (63%)
  waiting for transfers between devices  247 us (15%)
  matrix products  204 us (13%)
  blocking collectives  85.1 us (5%)
  other arithmetic  28.6 us (2%)
    gather x2, local copies, waits for them, and re-layouts, forward_item(): table_float[:, bucket]  934 us
    reduce_scatter x1, waiting for transfers between devices, on_device(): lax.psum_scatter(grad_down, ('dp', 'fsdp'), scatter_dimension=0, tiled=True)  142 us
    reduce_scatter x1, waiting for transfers between devices, on_device(): lax.psum_scatter(grad_up, ('dp', 'fsdp'), scatter_dimension=0, tiled=True)  102 us
    dot_general x8, matrix products, one_block(): jnp.dot(score_block, indicator, preferred_element_type=jnp.float32)  93.1 us
    unnamed x2, blocking collectives  85.1 us
    unnamed x77, local copies, waits for them, and re-layouts  33.7 us
  transfers between devices with their start and end apart: 8, of which 2 were waited for; matrix products, arithmetic and copies ran while one was open for 76% of the time, Pallas kernels for 0%

commit v1 on v0

v1 whole, which is shorter than its diff:
```python
import functools

import jax
import jax.numpy as jnp
from jax import lax
from jax.experimental import pallas as pl
from jax.experimental.pallas import tpu as pltpu
from jax.sharding import PartitionSpec as P

BF = jnp.bfloat16
F32 = jnp.float32
AXES = ("dp", "fsdp")
TILE = 128
CHUNK = 64
VMEM_BYTES = 56 * 1024 * 1024
EPS = 1e-05
NN = (((1,), (0,)), ((), ()))
NT = (((1,), (1,)), ((), ()))
TN = (((0,), (0,)), ((), ()))
VMEM = pltpu.VMEM


def mm(left, right, dims=NN):
    return lax.dot_general(left, right, dims, preferred_element_type=F32)


def any_spec():
    return pl.BlockSpec(memory_space=pl.ANY)


def smem_spec():
    return pl.BlockSpec(memory_space=pltpu.SMEM)


def whole(shape):
    return pl.BlockSpec(shape, lambda *_: (0,) * len(shape))


def params(grid_dims=1):
    return pltpu.CompilerParams(
        dimension_semantics=("arbitrary",) * grid_dims, vmem_limit_bytes=VMEM_BYTES
    )


def cost(flops, moved):
    return pl.CostEstimate(flops=int(flops), bytes_accessed=int(moved), transcendentals=0)


class Pieces:
    def __init__(self, buffers, offsets, rows):
        self.buffers = buffers
        self.offsets = offsets
        self.rows = rows

    @property
    def slots(self):
        return sum(b.shape[0] for b in self.buffers)


def load_copies(refs, offs_ref, rows, picks, sems):
    copies, slot, count = [], 0, 0
    for ref in refs:
        for k in range(ref.shape[0]):
            at = pl.multiple_of(offs_ref[slot], 16)
            for first, target in picks:
                copies.append(
                    pltpu.make_async_copy(
                        ref.at[k, pl.ds(first, rows)], target.at[pl.ds(at, rows)], sems.at[count]
                    )
                )
                count += 1
            slot += 1
    return copies


def row_norm(x):
    centre = x - jnp.mean(x, -1, keepdims=True)
    scale = lax.rsqrt(jnp.mean(centre * centre, -1, keepdims=True) + EPS)
    return centre * scale, scale


def bias_tiles(curve):
    heads, span = curve.shape
    tiles = span // TILE - 1

    def kernel(curve_ref, out_ref):
        base = pltpu.roll(jnp.broadcast_to(curve_ref[0], (8, span)), 0, 1, stride=1, stride_axis=0)
        for pair in range(TILE // 16):
            rolled = jnp.concatenate(
                [pltpu.roll(base, 16 * pair + 8 * i, 1) if pair + i else base for i in range(2)], 0
            ).astype(BF)
            for d in range(tiles):
                out_ref[0, d, 16 * pair : 16 * pair + 16, :] = rolled[
                    :, TILE * (d + 1) : TILE * (d + 2)
                ]

    return pl.pallas_call(
        kernel,
        grid=(heads,),
        in_specs=[pl.BlockSpec((1, 1, span), lambda h: (h, 0, 0))],
        out_specs=pl.BlockSpec((1, tiles, TILE, TILE), lambda h: (h, 0, 0, 0)),
        out_shape=jax.ShapeDtypeStruct((heads, tiles, TILE, TILE), BF),
        compiler_params=params(),
        name="bias_tiles",
    )(curve.reshape(heads, 1, span))


def place_rows(block, offset, wide):
    padded = jnp.concatenate([block, jnp.zeros((block.shape[0], wide - TILE), block.dtype)], 1)
    return pltpu.roll(padded, offset, 1)


def attention_forward(half, core, tokens, normed, vec, pieces, tiles, lengths, head_size, tokens_in=()):
    rows, model = tokens.shape if normed is None else normed.shape
    width = model // 2
    heads = width // head_size
    pairs = width // TILE
    per = TILE // head_size
    first = normed is None
    unpack = vec is None
    n_buf = len(pieces.buffers)
    slots = pieces.slots
    scale = head_size**-0.5

    def kernel(core_ref, offs_ref, len_ref, x_ref, *refs):
        if not unpack:
            vec_ref, refs = refs[0], refs[1:]
        tile_ref, bufs, rest = refs[0], refs[1 : 1 + n_buf], refs[1 + n_buf + len(tokens_in) :]
        if first:
            n1_ref, rest = rest[0], rest[1:]
        if unpack:
            vec_ref, rest = rest[0], rest[1:]
        joined_ref, mixed_ref, p_ref, w_ref, qs_ref, s_ref, raw_ref, sems = rest
        pair = pl.program_id(0)

        @pl.when(pair == 0)
        def _():
            copies = load_copies(
                bufs, offs_ref, pieces.rows, [(j * pieces.rows, w_ref.at[j]) for j in range(3)], sems
            )
            if unpack:
                small, slot = [], 0
                for ref in bufs:
                    for k in range(ref.shape[0]):
                        small.append(
                            pltpu.make_async_copy(
                                ref.at[k, pl.ds(4 * pieces.rows, 16), pl.ds(0, TILE)],
                                raw_ref.at[slot],
                                sems.at[3 * slots + slot],
                            )
                        )
                        slot += 1
                for c in small:
                    c.start()
            for c in copies:
                c.start()
            if unpack:
                for c in small:
                    c.wait()
                total = jnp.zeros((16, model), F32)
                for slot in range(slots):
                    total += place_rows(raw_ref[slot].astype(F32), offs_ref[slot], model)
                vec_ref[...] = total
            if first:
                for r in range(0, rows, CHUNK):
                    xhat, _ = row_norm(x_ref[r : r + CHUNK, :].astype(F32))
                    n1_ref[r : r + CHUNK, :] = (xhat * vec_ref[0:1, :] + vec_ref[1:2, :]).astype(BF)
            for c in copies:
                c.wait()
            src = n1_ref if first else x_ref
            cols = pl.ds(pl.multiple_of((core_ref[0] ^ half) * width, TILE), width)
            for j in range(3):
                joined = mm(src[...], w_ref[j])
                if j != 1:
                    joined = joined + vec_ref[2 + j // 2 : 3 + j // 2, cols]
                qs_ref[j] = joined.astype(BF)

        lanes = pl.ds(pl.multiple_of(pair * TILE, TILE), TILE)
        q, k, v = (qs_ref[j, :, lanes] for j in range(3))
        for j, one in enumerate((q, k, v)):
            joined_ref[j] = one
        lane = lax.broadcasted_iota(jnp.int32, (1, TILE), 1)
        column = lax.broadcasted_iota(jnp.int32, (1, rows), 1)
        dead = jnp.where(column < len_ref[0], 0.0, -1e30).astype(F32)
        scaled = q.astype(F32) * scale
        outs = []
        for e in range(per):
            mine = (lane >= e * head_size) & (lane < (e + 1) * head_size)
            qm = jnp.where(mine, scaled, 0.0).astype(BF)
            s_ref[e] = mm(qm, k, NT)
            for r in range(0, rows, CHUNK):
                block, sub = r // TILE, r % TILE
                rel = jnp.concatenate(
                    [
                        tile_ref[e, j - block + rows // TILE - 1, sub : sub + CHUNK, :]
                        for j in range(rows // TILE)
                    ],
                    1,
                ).astype(F32)
                s = s_ref[e, r : r + CHUNK, :] + (rel + dead)
                raised = jnp.exp(s - jnp.max(s, -1, keepdims=True))
                inv = 1.0 / jnp.sum(raised, -1, keepdims=True)
                p_ref[e, r : r + CHUNK, :] = (raised * inv).astype(BF)
            outs.append(jnp.where(mine, mm(p_ref[e], v), 0.0))
        mixed_ref[...] = functools.reduce(lambda a, b: a + b, outs).astype(BF)

    ins = [core, pieces.offsets, lengths, tokens if first else normed]
    specs = [smem_spec(), smem_spec(), smem_spec(), whole((rows, model))]
    if not unpack:
        ins.append(vec)
        specs.append(whole((16, model)))
    tiles_n = tiles.shape[1]
    ins += [tiles, *pieces.buffers, *tokens_in]
    base = half * (heads // per)
    specs += [
        pl.BlockSpec((per, tiles_n, TILE, TILE), lambda p: (base + p, 0, 0, 0)),
        *[any_spec()] * (n_buf + len(tokens_in)),
    ]
    shapes = [
        jax.ShapeDtypeStruct((3, rows, width), BF),
        jax.ShapeDtypeStruct((rows, width), BF),
        jax.ShapeDtypeStruct((heads, rows, rows), BF),
    ]
    outs = [
        pl.BlockSpec((3, rows, TILE), lambda p: (0, 0, p)),
        pl.BlockSpec((rows, TILE), lambda p: (0, p)),
        pl.BlockSpec((per, rows, rows), lambda p: (p, 0, 0)),
    ]
    if unpack:
        shapes.insert(0, jax.ShapeDtypeStruct((16, model), F32))
        outs.insert(0, whole((16, model)))
    if first:
        shapes.insert(0, jax.ShapeDtypeStruct((rows, model), BF))
        outs.insert(0, whole((rows, model)))
    return pl.pallas_call(
        kernel,
        grid=(pairs,),
        in_specs=specs,
        out_specs=outs,
        out_shape=shapes,
        scratch_shapes=[
            VMEM((3, model, width), BF),
            VMEM((3, rows, width), BF),
            VMEM((per, rows, rows), F32),
            VMEM((slots, 16, TILE), BF),
            pltpu.SemaphoreType.DMA((4 * slots,)),
        ],
        compiler_params=params(),
        cost_estimate=cost(2e9, 1e7),
        name="attention_forward",
    )(*ins)


def project_out(core, mixed, tokens, pieces, vec, tokens_in=()):
    rows, model = tokens.shape
    width = model // 2
    sizes = [len(p.buffers) for p in pieces]
    per = [p.slots for p in pieces]

    def kernel(core_ref, offs0, offs1, m0_ref, m1_ref, x_ref, vec_ref, *rest):
        bufs = [rest[: sizes[0]], rest[sizes[0] : sum(sizes)]]
        res_ref, n2_ref, w_ref, sems = rest[sum(sizes) + len(tokens_in) :]
        copies = []
        for h, offs in enumerate((offs0, offs1)):
            copies += load_copies(
                bufs[h], offs, pieces[h].rows, [(3 * pieces[h].rows, w_ref.at[h])],
                sems.at[pl.ds(h * per[0], per[h])],
            )
        for c in copies:
            c.start()
        for c in copies:
            c.wait()
        for h in range(2):
            cols = pl.ds(pl.multiple_of((core_ref[0] ^ h) * width, TILE), width)
            acc = 0.0
            for g, m_ref in enumerate((m0_ref, m1_ref)):
                feats = pl.ds(pl.multiple_of((core_ref[0] ^ g) * width, TILE), width)
                acc = acc + mm(m_ref[...], w_ref[h, feats, :])
            res_ref[:, cols] = x_ref[:, cols].astype(F32) + acc + vec_ref[4:5, cols]
        for r in range(0, rows, CHUNK):
            xhat, _ = row_norm(res_ref[r : r + CHUNK, :])
            n2_ref[r : r + CHUNK, :] = (xhat * vec_ref[5:6, :] + vec_ref[6:7, :]).astype(BF)

    return pl.pallas_call(
        kernel,
        grid=(1,),
        in_specs=[
            *[smem_spec()] * 3,
            whole((rows, width)),
            whole((rows, width)),
            whole((rows, model)),
            whole((16, model)),
            *[any_spec()] * (sum(sizes) + len(tokens_in)),
        ],
        out_specs=[whole((rows, model)), whole((rows, model))],
        out_shape=[
            jax.ShapeDtypeStruct((rows, model), F32),
            jax.ShapeDtypeStruct((rows, model), BF),
        ],
        scratch_shapes=[VMEM((2, model, width), BF), pltpu.SemaphoreType.DMA((sum(per),))],
        compiler_params=params(),
        cost_estimate=cost(6e8, 5e6),
        name="project_out",
    )(
        core, pieces[0].offsets, pieces[1].offsets, mixed[0], mixed[1], tokens, vec,
        *pieces[0].buffers, *pieces[1].buffers, *tokens_in,
    )


def feed_forward(part, core, normed, grad_rows, vec, pieces, result_in, grad_in, tokens_in=()):
    rows, model = normed.shape
    hidden = model
    sizes = [len(p.buffers) for p in pieces]
    per = [p.slots for p in pieces]
    first = grad_in is None
    step_rows = rows // 2

    def kernel(core_ref, offs0, offs1, n_ref, gr_ref, vec_ref, res_ref, *rest):
        if not first:
            gin_ref, rest = rest[0], rest[1:]
        bufs = [rest[: sizes[0]], rest[sizes[0] : sum(sizes)]]
        out_ref, gn_ref, act_ref, gp_ref, col_ref, up_ref, down_ref, sems = rest[
            sum(sizes) + len(tokens_in) :
        ]
        step = pl.program_id(0)

        def copies(h):
            return load_copies(
                bufs[h], (offs0, offs1)[h], pieces[h].rows,
                [(0, up_ref.at[h]), (pieces[h].rows, down_ref.at[h])],
                sems.at[pl.ds(2 * h * per[0], 2 * per[h])],
            )

        @pl.when(step == 0)
        def _():
            both = [copies(0), copies(1)]
            for c in both[0] + both[1]:
                c.start()
            if first:
                out_ref[...] = res_ref[...] + vec_ref[7:8, :]
                gn_ref[...] = jnp.zeros_like(gn_ref)
            else:
                out_ref[...] = res_ref[...]
                gn_ref[...] = gin_ref[...]
            for c in both[0]:
                c.wait()

        @pl.when(step == 1)
        def _():
            for c in copies(1):
                c.wait()

        sums = jnp.zeros((1, hidden), F32)
        up_bias = vec_ref[pl.ds(8 + 2 * part + (core_ref[0] ^ step), 1), :]
        for r in range(0, rows, step_rows):
            block = slice(r, r + step_rows)
            pre = mm(n_ref[block, :], up_ref[step]) + up_bias
            gact = mm(gr_ref[block, :], down_ref[step], NT)
            cdf = 0.5 * (1.0 + lax.erf(pre * 0.7071067811865476))
            act = (pre * cdf).astype(BF)
            slope = cdf + pre * (jnp.exp(-0.5 * (pre * pre)) * 0.3989422804014327)
            gp = (gact * slope).astype(BF)
            act_ref[0, block, :] = act
            gp_ref[0, block, :] = gp
            sums += jnp.sum(gp.astype(F32), 0, keepdims=True)
            out_ref[block, :] += mm(act, down_ref[step])
            gn_ref[block, :] += mm(gp, up_ref[step], NT)
        col_ref[0] = sums

    ins = [core, pieces[0].offsets, pieces[1].offsets, normed, grad_rows, vec, result_in]
    specs = [
        *[smem_spec()] * 3, whole((rows, model)), whole((rows, model)),
        whole((16, model)), whole((rows, model)),
    ]
    if not first:
        ins.append(grad_in)
        specs.append(whole((rows, model)))
    return pl.pallas_call(
        kernel,
        grid=(2,),
        in_specs=specs + [any_spec()] * (sum(sizes) + len(tokens_in)),
        out_specs=[
            whole((rows, model)),
            whole((rows, model)),
            pl.BlockSpec((1, rows, hidden), lambda s: (s, 0, 0)),
            pl.BlockSpec((1, rows, hidden), lambda s: (s, 0, 0)),
            pl.BlockSpec((1, 1, hidden), lambda s: (s, 0, 0)),
        ],
        out_shape=[
            jax.ShapeDtypeStruct((rows, model), F32),
            jax.ShapeDtypeStruct((rows, model), F32),
            jax.ShapeDtypeStruct((2, rows, hidden), BF),
            jax.ShapeDtypeStruct((2, rows, hidden), BF),
            jax.ShapeDtypeStruct((2, 1, hidden), F32),
        ],
        scratch_shapes=[
            VMEM((2, model, hidden), BF),
            VMEM((2, hidden, model), BF),
            pltpu.SemaphoreType.DMA((2 * sum(per),)),
        ],
        compiler_params=params(),
        cost_estimate=cost(6.4e9, 2e7),
        name="feed_forward",
    )(*ins, *pieces[0].buffers, *pieces[1].buffers, *tokens_in)


def outer_products(pairs, offsets, rows, extra=None, tokens_in=()):
    counts = [len(lefts) for lefts, _ in pairs]
    slots = offsets.shape[0]
    half = max(slots // 2, 1)
    wide = pairs[0][1][0][0].shape[-1]
    tall = pairs[0][0][0][0].shape[-1]
    tail = 0 if extra is None else 32
    n_mat = len(pairs)
    flat, where = [], []
    for lefts, rights in pairs:
        places = []
        for one, lead in (*lefts, *rights):
            match = [i for i, known in enumerate(flat) if known is one]
            if not match:
                flat.append(one)
                match = [len(flat) - 1]
            places.append((match[0], lead))
        where.append(places)

    def kernel(offs_ref, *rest):
        ins = rest[: len(flat)]
        rest = rest[len(flat) :]
        if tail:
            vec_ref, table_ref, rest = rest[0], rest[1], rest[2:]
        rest = rest[len(tokens_in) :]
        keep_ref = rest[0]
        send_ref = rest[1] if slots > 1 else None
        w_ref, tail_ref, sems = rest[-3:]
        copies = [[] for _ in range(n_mat + 1)]
        count = 0
        for s in range(slots):
            at = pl.multiple_of(offs_ref[s], 16)
            out_ref = (keep_ref if s < half else send_ref).at[s % half]
            for m in range(n_mat):
                copies[m].append(
                    pltpu.make_async_copy(
                        w_ref.at[m, pl.ds(at, rows)], out_ref.at[pl.ds(m * rows, rows)], sems.at[count]
                    )
                )
                count += 1
            if tail:
                copies[n_mat].append(
                    pltpu.make_async_copy(
                        tail_ref.at[s], out_ref.at[pl.ds(n_mat * rows, tail)], sems.at[count]
                    )
                )
                count += 1
        if tail:
            model = vec_ref.shape[1]
            table = table_ref[...]
            for s in range(slots):
                small = pltpu.roll(vec_ref[...], lax.rem(model - offs_ref[s], model), 1)[:, :TILE]
                tail_ref[s] = jnp.concatenate(
                    [jnp.concatenate([small, table[:16, TILE:]], 1), table[16:]], 0
                ).astype(BF)
            for c in copies[n_mat]:
                c.start()
        for m in range(n_mat):
            places = where[m]
            total = 0.0
            for i in range(counts[m]):
                left, right = (
                    ins[at][...] if lead is None else ins[at][lead]
                    for at, lead in (places[i], places[counts[m] + i])
                )
                total = total + mm(left, right, TN)
            w_ref[m] = total.astype(BF)
            for c in copies[m]:
                c.start()
        for group in copies:
            for c in group:
                c.wait()

    ins = [offsets, *flat]
    specs = [smem_spec(), *[whole(one.shape) for one in flat]]
    if tail:
        ins += list(extra)
        specs += [whole(one.shape) for one in extra]
    ins += list(tokens_in)
    specs += [any_spec()] * len(tokens_in)
    shape = jax.ShapeDtypeStruct((half, n_mat * rows + tail, wide), BF)
    n_out = 2 if slots > 1 else 1
    return pl.pallas_call(
        kernel,
        grid=(1,),
        in_specs=specs,
        out_specs=[any_spec()] * n_out,
        out_shape=[shape] * n_out,
        scratch_shapes=[
            VMEM((n_mat, tall, wide), BF),
            VMEM((slots, 32, wide), BF),
            pltpu.SemaphoreType.DMA((slots * (n_mat + 1),)),
        ],
        compiler_params=params(),
        cost_estimate=cost(2e9, 1e7),
        name="outer_products",
    )(*ins)


def norm_back(x, up, gain):
    xhat, scale = row_norm(x)
    e = up * gain
    grad = scale * (e - jnp.mean(e, -1, keepdims=True) - xhat * jnp.mean(e * xhat, -1, keepdims=True))
    return grad, up * xhat


def second_norm_back(core, residual, result, grad_normed, grad_rows, pieces, vec, lengths, tokens_in=()):
    rows, model = residual.shape
    width = model // 2
    sizes = [len(p.buffers) for p in pieces]
    per = [p.slots for p in pieces]

    def kernel(core_ref, len_ref, offs0, offs1, res_ref, out_in, gn_ref, gr_ref, vec_ref, *rest):
        bufs = [rest[: sizes[0]], rest[sizes[0] : sum(sizes)]]
        out_ref, gres_ref, gb_ref, gm0_ref, gm1_ref, sums_ref, w_ref, sems = rest[
            sum(sizes) + len(tokens_in) :
        ]
        copies = []
        for h, offs in enumerate((offs0, offs1)):
            copies += load_copies(
                bufs[h], offs, pieces[h].rows, [(3 * pieces[h].rows, w_ref.at[h])],
                sems.at[pl.ds(h * per[0], per[h])],
            )
        for c in copies:
            c.start()
        totals = [jnp.zeros((1, model), F32) for _ in range(4)]
        for r in range(0, rows, CHUNK):
            block = slice(r, r + CHUNK)
            row = lax.broadcasted_iota(jnp.int32, (CHUNK, 1), 0) + r
            out_ref[block, :] = jnp.where(row < len_ref[0], out_in[block, :], 0.0).astype(BF)
            up = gn_ref[block, :]
            grad, gain_terms = norm_back(res_ref[block, :], up, vec_ref[5:6, :])
            gr = gr_ref[block, :].astype(F32)
            grad = gr + grad
            low = grad.astype(BF)
            gres_ref[block, :] = grad
            gb_ref[block, :] = low
            for i, terms in enumerate((gain_terms, up, low.astype(F32), gr)):
                totals[i] += jnp.sum(terms, 0, keepdims=True)
        sums_ref[...] = jnp.concatenate(totals + [jnp.zeros((4, model), F32)], 0)
        for c in copies:
            c.wait()
        for h, gm_ref in enumerate((gm0_ref, gm1_ref)):
            feats = pl.ds(pl.multiple_of((core_ref[0] ^ h) * width, TILE), width)
            acc = 0.0
            for g in range(2):
                cols = pl.ds(pl.multiple_of((core_ref[0] ^ g) * width, TILE), width)
                acc = acc + mm(gb_ref[:, cols], w_ref[g, feats, :], NT)
            gm_ref[...] = acc.astype(BF)

    return pl.pallas_call(
        kernel,
        grid=(1,),
        in_specs=[
            *[smem_spec()] * 4,
            *[whole((rows, model))] * 4,
            whole((16, model)),
            *[any_spec()] * (sum(sizes) + len(tokens_in)),
        ],
        out_specs=[
            *[whole((rows, model))] * 3,
            *[whole((rows, width))] * 2,
            whole((8, model)),
        ],
        out_shape=[
            jax.ShapeDtypeStruct((rows, model), BF),
            jax.ShapeDtypeStruct((rows, model), F32),
            jax.ShapeDtypeStruct((rows, model), BF),
            jax.ShapeDtypeStruct((rows, width), BF),
            jax.ShapeDtypeStruct((rows, width), BF),
            jax.ShapeDtypeStruct((8, model), F32),
        ],
        scratch_shapes=[VMEM((2, model, width), BF), pltpu.SemaphoreType.DMA((sum(per),))],
        compiler_params=params(),
        cost_estimate=cost(6e8, 1e7),
        name="second_norm_back",
    )(
        core, lengths, pieces[0].offsets, pieces[1].offsets, residual, result, grad_normed, grad_rows,
        vec, *pieces[0].buffers, *pieces[1].buffers, *tokens_in,
    )


def attention_backward(joined, probs, mixed, grad_mixed, head_size, tokens_in=()):
    _, rows, width = joined.shape
    heads = width // head_size
    pairs = width // TILE
    per = TILE // head_size
    tiles = 2 * (rows // TILE) - 1
    span = 2 * rows
    scale = head_size**-0.5

    def kernel(joined_ref, p_ref, mixed_ref, gm_ref, *rest):
        out_ref, diag_ref, gp_ref, ds_ref, acc_ref = rest[len(tokens_in) :]
        q, k, v = joined_ref[0], joined_ref[1], joined_ref[2]
        gm = gm_ref[...]
        lane = lax.broadcasted_iota(jnp.int32, (1, TILE), 1)
        dots = gm.astype(F32) * mixed_ref[...].astype(F32)
        q_t, gm_t = q.T, gm.T
        dq, dk, dv = [], [], []
        for e in range(per):
            mine = (lane >= e * head_size) & (lane < (e + 1) * head_size)
            feats = slice(e * head_size, (e + 1) * head_size)
            delta = jnp.sum(jnp.where(mine, dots, 0.0), -1, keepdims=True)
            gp_ref[e] = mm(jnp.where(mine, gm, jnp.zeros_like(gm)), v, NT)
            acc_ref[...] = jnp.zeros_like(acc_ref)
            for r in range(0, rows, CHUNK):
                block, sub = r // TILE, r % TILE
                ds = p_ref[e, r : r + CHUNK, :].astype(F32) * (
                    gp_ref[e, r : r + CHUNK, :] - delta[r : r + CHUNK, :]
                )
                ds_ref[e, r : r + CHUNK, :] = ds.astype(BF)
                for j in range(rows // TILE):
                    acc_ref[j - block + rows // TILE - 1, sub : sub + CHUNK, :] += ds[
                        :, j * TILE : (j + 1) * TILE
                    ]
            dq.append(jnp.where(mine, mm(ds_ref[e], k), 0.0))
            dk.append(mm(q_t[feats, :], ds_ref[e]))
            dv.append(mm(gm_t[feats, :], p_ref[e]))
            total = jnp.zeros((8, span), F32)
            for g in range(TILE // 8):
                strip = jnp.concatenate(
                    [jnp.zeros((8, TILE), F32)]
                    + [acc_ref[d, 8 * g : 8 * g + 8, :] for d in range(tiles)],
                    1,
                )
                total += pltpu.roll(strip, (span - 8 * g) % span, 1) if g else strip
            line = total[0:1]
            for i in range(1, 8):
                line = line + pltpu.roll(total[i : i + 1], span - i, 1)
            diag_ref[e] = line
        out_ref[0] = (functools.reduce(lambda a, b: a + b, dq) * scale).astype(BF)
        out_ref[1] = (jnp.concatenate(dk, 0) * scale).T.astype(BF)
        out_ref[2] = jnp.concatenate(dv, 0).T.astype(BF)

    return pl.pallas_call(
        kernel,
        grid=(pairs,),
        in_specs=[
            pl.BlockSpec((3, rows, TILE), lambda p: (0, 0, p)),
            pl.BlockSpec((per, rows, rows), lambda p: (p, 0, 0)),
            pl.BlockSpec((rows, TILE), lambda p: (0, p)),
            pl.BlockSpec((rows, TILE), lambda p: (0, p)),
            *[any_spec()] * len(tokens_in),
        ],
        out_specs=[
            pl.BlockSpec((3, rows, TILE), lambda p: (0, 0, p)),
            pl.BlockSpec((per, 1, span), lambda p: (p, 0, 0)),
        ],
        out_shape=[
            jax.ShapeDtypeStruct((3, rows, width), BF),
            jax.ShapeDtypeStruct((heads, 1, span), F32),
        ],
        scratch_shapes=[
            VMEM((per, rows, rows), F32),
            VMEM((per, rows, rows), BF),
            VMEM((tiles, TILE, TILE), F32),
        ],
        compiler_params=params(),
        cost_estimate=cost(4e9, 1e7),
        name="attention_backward",
    )(joined, probs, mixed, grad_mixed, *tokens_in)


def first_norm_back(core, grads, tokens, grad_residual, vec, pieces, sums_second, sums_up, diags, chosen, tokens_in=()):
    rows, model = tokens.shape
    width = model // 2
    heads = diags[0].shape[0]
    number, span = chosen.shape
    sizes = [len(p.buffers) for p in pieces]
    per = [p.slots for p in pieces]

    def kernel(core_ref, offs0, offs1, d0_ref, d1_ref, x_ref, gres_ref, vec_ref, s2_ref, u0_ref, u1_ref, t0_ref,
               t1_ref, chosen_ref, *rest):
        bufs = [rest[: sizes[0]], rest[sizes[0] : sum(sizes)]]
        gx_ref, sums_ref, table_ref, w_ref, acc_ref, sems = rest[sum(sizes) + len(tokens_in) :]
        groups = []
        for h, offs in enumerate((offs0, offs1)):
            groups.append(
                load_copies(
                    bufs[h], offs, pieces[h].rows,
                    [(j * pieces[h].rows, w_ref.at[h, j]) for j in range(3)],
                    sems.at[pl.ds(3 * h * per[0], 3 * per[h])],
                )
            )
        for c in groups[0] + groups[1]:
            c.start()
        straight = core_ref[0] == 0

        def ordered(a, b):
            return [jnp.where(straight, a, b), jnp.where(straight, b, a)]

        diag = jnp.concatenate(ordered(t0_ref[:, 0, :], t1_ref[:, 0, :]) + [jnp.zeros((16 - 2 * heads, span), F32)], 0)
        table, left = 0.0, diag
        for _ in range(3):
            part = left.astype(BF)
            table = table + mm(part, chosen_ref[...], NT)
            left = left - part.astype(F32)
        table = jnp.concatenate([table, jnp.zeros((16, 2 * width - number), F32)], 1)
        table_ref[...] = jnp.concatenate(
            [
                jnp.concatenate([jnp.zeros((16, TILE), F32), table[:, width : 2 * width - TILE]], 1),
                table[:, :width],
            ],
            0,
        )
        columns = [
            jnp.concatenate(
                ordered(*(jnp.sum(d_ref[j].astype(F32), 0, keepdims=True) for d_ref in (d0_ref, d1_ref))), 1
            )
            for j in (0, 2)
        ]
        for c in groups[0] + groups[1]:
            c.wait()
        acc = 0.0
        for h, d_ref in enumerate((d0_ref, d1_ref)):
            for j in range(3):
                acc = acc + mm(d_ref[j], w_ref[h, j], NT)
        acc_ref[...] = acc
        totals = [jnp.zeros((1, model), F32) for _ in range(2)]
        for r in range(0, rows, CHUNK):
            block = slice(r, r + CHUNK)
            up = acc_ref[block, :]
            grad, gain_terms = norm_back(x_ref[block, :].astype(F32), up, vec_ref[0:1, :])
            gx_ref[block, :] = gres_ref[block, :] + grad
            totals[0] += jnp.sum(gain_terms, 0, keepdims=True)
            totals[1] += jnp.sum(up, 0, keepdims=True)
        sums_ref[...] = jnp.concatenate(
            totals
            + columns
            + [s2_ref[2:3, :], s2_ref[0:1, :], s2_ref[1:2, :], s2_ref[3:4, :]]
            + ordered(u0_ref[0], u0_ref[1])
            + ordered(u1_ref[0], u1_ref[1])
            + [jnp.zeros((4, model), F32)],
            0,
        )

    return pl.pallas_call(
        kernel,
        grid=(1,),
        in_specs=[
            *[smem_spec()] * 3,
            whole((3, rows, width)),
            whole((3, rows, width)),
            whole((rows, model)),
            whole((rows, model)),
            whole((16, model)),
            whole((8, model)),
            whole((2, 1, model)),
            whole((2, 1, model)),
            whole((heads, 1, span)),
            whole((heads, 1, span)),
            whole((number, span)),
            *[any_spec()] * (sum(sizes) + len(tokens_in)),
        ],
        out_specs=[whole((rows, model)), whole((16, model)), whole((32, width))],
        out_shape=[
            jax.ShapeDtypeStruct((rows, model), F32),
            jax.ShapeDtypeStruct((16, model), F32),
            jax.ShapeDtypeStruct((32, width), F32),
        ],
        scratch_shapes=[
            VMEM((2, 3, model, width), BF),
            VMEM((rows, model), F32),
            pltpu.SemaphoreType.DMA((3 * sum(per),)),
        ],
        compiler_params=params(),
        cost_estimate=cost(2e9, 1e7),
        name="first_norm_back",
    )(
        core, pieces[0].offsets, pieces[1].offsets, grads[0], grads[1], tokens, grad_residual, vec, sums_second,
        *sums_up, *diags, chosen, *pieces[0].buffers, *pieces[1].buffers, *tokens_in,
    )


def pack_blocks(core, qkv, out, up):
    local, model = out.shape
    width = model // 2
    n_up = up.shape[1]
    owners = n_up // (4 * model)
    del owners
    unit = local * 2
    chips = n_up // (4 * unit)

    def kernel(core_ref, qkv_ref, out_ref, up_ref, a0_ref, a1_ref, u0_ref, u1_ref):
        core_at = core_ref[0]
        for h, (a_ref, u_ref) in enumerate(((a0_ref, u0_ref), (a1_ref, u1_ref))):
            at = (core_at ^ h) * width
            for j in range(3):
                a_ref[j] = qkv_ref[:, pl.ds(pl.multiple_of(j * model + at, TILE), width)]
            a_ref[3] = out_ref[:, pl.ds(pl.multiple_of(at, TILE), width)]
        for f in range(2):
            by_core = []
            for c in range(2):
                by_core.append(
                    jnp.concatenate(
                        [
                            up_ref[:, ((2 * chip + c) * 2 + f) * unit : ((2 * chip + c) * 2 + f + 1) * unit]
                            for chip in range(chips)
                        ],
                        1,
                    ).astype(F32)
                )
            first = core_at == 0
            u0_ref[f] = jnp.where(first, by_core[0], by_core[1]).astype(BF)
            u1_ref[f] = jnp.where(first, by_core[1], by_core[0]).astype(BF)

    shapes = [jax.ShapeDtypeStruct((4, local, width), BF)] * 2 + [jax.ShapeDtypeStruct((2, local, model), BF)] * 2
    return pl.pallas_call(
        kernel,
        grid=(1,),
        in_specs=[smem_spec(), whole(qkv.shape), whole(out.shape), whole(up.shape)],
        out_specs=[whole(one.shape) for one in shapes],
        out_shape=shapes,
        compiler_params=params(),
        name="pack_blocks",
    )(core, qkv, out, up)


def ordered_rows(core_at, mine, theirs):
    first = core_at == 0
    a, b = mine.astype(F32), theirs.astype(F32)
    return jnp.concatenate([jnp.where(first, a, b), jnp.where(first, b, a)], 0)


def merge_attention(core, mine, theirs, small, small_theirs):
    count, local, width = mine.shape

    def kernel(core_ref, a_ref, b_ref, s_ref, t_ref, out_ref):
        for j in range(count):
            out_ref[2 * local * j : 2 * local * (j + 1), :] = ordered_rows(core_ref[0], a_ref[j], b_ref[j]).astype(BF)
        vec = s_ref[...].astype(F32) + t_ref[...].astype(F32)
        out_ref[2 * local * count :, :] = jnp.concatenate([vec, jnp.zeros((16, width - TILE), F32)], 1).astype(BF)

    return pl.pallas_call(
        kernel,
        grid=(1,),
        in_specs=[smem_spec(), *[whole(mine.shape)] * 2, *[whole(small.shape)] * 2],
        out_specs=whole((2 * local * count + 16, width)),
        out_shape=jax.ShapeDtypeStruct((2 * local * count + 16, width), BF),
        compiler_params=params(),
        name="merge_attention",
    )(core, mine, theirs, small, small_theirs)


def merge_feed_forward(core, mine, theirs, down):
    _, local, model = mine.shape
    unit = 2 * local

    def kernel(core_ref, a_ref, b_ref, d_ref, *outs):
        for f in range(2):
            outs[f][:unit, :] = ordered_rows(core_ref[0], a_ref[f], b_ref[f]).astype(BF)
            outs[f][unit:, :] = d_ref[f * unit : (f + 1) * unit, :]

    shape = jax.ShapeDtypeStruct((2 * unit, model), BF)
    return pl.pallas_call(
        kernel,
        grid=(1,),
        in_specs=[smem_spec(), *[whole(mine.shape)] * 2, whole(down.shape)],
        out_specs=[whole(shape.shape)] * 2,
        out_shape=[shape] * 2,
        compiler_params=params(),
        name="merge_feed_forward",
    )(core, mine, theirs, down)


def pair_sum(refs):
    parts = [ref[...].astype(F32) for ref in refs]
    while len(parts) > 1:
        half = len(parts) // 2
        parts = [parts[i] + parts[i + half] for i in range(half)]
    return parts[0]


def rows_of(total, first, core_at, local, mine):
    a, b = total[first : first + local], total[first + local : first + 2 * local]
    return jnp.where((core_at == 0) == mine, a, b)


def total_attention(core, parts, local):
    tall, width = parts[0].shape
    tail = tall - 8 * local

    def kernel(core_ref, *refs):
        ins, (mine_ref, sent_ref, tail_ref) = refs[: len(parts)], refs[len(parts) :]
        total = pair_sum(ins)
        for j in range(4):
            mine_ref[j] = rows_of(total, 2 * local * j, core_ref[0], local, True)
            sent_ref[j] = rows_of(total, 2 * local * j, core_ref[0], local, False).astype(BF)
        tail_ref[...] = total[8 * local :].astype(BF)

    shapes = [
        jax.ShapeDtypeStruct((4, local, width), F32),
        jax.ShapeDtypeStruct((4, local, width), BF),
        jax.ShapeDtypeStruct((tail, width), BF),
    ]
    return pl.pallas_call(
        kernel,
        grid=(1,),
        in_specs=[smem_spec(), *[whole(one.shape) for one in parts]],
        out_specs=[whole(one.shape) for one in shapes],
        out_shape=shapes,
        compiler_params=params(),
        name="total_attention",
    )(core, *parts)


def finish_attention(core, mine, theirs, tail, tail_theirs, heads, number):
    _, local, width = mine.shape
    model = 2 * width

    def kernel(core_ref, a_ref, b_ref, s_ref, t_ref, qkv_ref, out_ref, small_ref, table_ref):
        at = core_ref[0]
        for h, ref in enumerate((a_ref, b_ref)):
            for j in range(3):
                cols = pl.ds(pl.multiple_of(j * model + (at ^ h) * width, TILE), width)
                qkv_ref[:, cols] = ref[j].astype(F32)
            out_ref[:, pl.ds(pl.multiple_of((at ^ h) * width, TILE), width)] = ref[3].astype(F32)
        total = s_ref[...].astype(F32) + t_ref[...].astype(F32)
        small = total[:16, :TILE]
        moved = pltpu.roll(small, TILE - local, 1)
        small_ref[:8, :] = jnp.where(at == 0, small[:8], moved[:8])
        small_ref[8:, :] = small[8:]
        table_ref[...] = jnp.concatenate([total[16:, :], total[:16, TILE : TILE + number - width]], 1)[:heads]

    shapes = [
        jax.ShapeDtypeStruct((local, 3 * model), F32),
        jax.ShapeDtypeStruct((local, model), F32),
        jax.ShapeDtypeStruct((16, TILE), F32),
        jax.ShapeDtypeStruct((heads, number), F32),
    ]
    return pl.pallas_call(
        kernel,
        grid=(1,),
        in_specs=[smem_spec(), *[whole(one.shape) for one in (mine, theirs, tail, tail_theirs)]],
        out_specs=[whole(one.shape) for one in shapes],
        out_shape=shapes,
        compiler_params=params(),
        name="finish_attention",
    )(core, mine, theirs, tail, tail_theirs)


def total_feed_forward(core, parts, local):
    _, model = parts[0].shape
    unit = 2 * local

    def kernel(core_ref, *refs):
        ins, (mine_ref, sent_ref, down_ref) = refs[: len(parts)], refs[len(parts) :]
        total = pair_sum(ins)
        mine_ref[...] = rows_of(total, 0, core_ref[0], local, True)
        sent_ref[...] = rows_of(total, 0, core_ref[0], local, False).astype(BF)
        down_ref[...] = total[unit:]

    shapes = [
        jax.ShapeDtypeStruct((local, model), F32),
        jax.ShapeDtypeStruct((local, model), BF),
        jax.ShapeDtypeStruct((unit, model), F32),
    ]
    return pl.pallas_call(
        kernel,
        grid=(1,),
        in_specs=[smem_spec(), *[whole(one.shape) for one in parts]],
        out_specs=[whole(one.shape) for one in shapes],
        out_shape=shapes,
        compiler_params=params(),
        name="total_feed_forward",
    )(core, *parts)


def finish_feed_forward(core, mine, theirs, downs):
    local, model = mine[0].shape
    unit = 2 * local
    chips = model // unit

    def kernel(core_ref, m0, m1, t0, t1, d0, d1, up_ref, down_ref):
        first = core_ref[0] == 0
        by = []
        for a, b in ((m0, t0), (m1, t1)):
            a, b = a[...], b[...].astype(F32)
            by.append((jnp.where(first, a, b), jnp.where(first, b, a)))
        up_ref[...] = jnp.concatenate(
            [
                by[f][c][:, chip * unit : (chip + 1) * unit]
                for chip in range(chips)
                for c in range(2)
                for f in range(2)
            ],
            1,
        )
        down_ref[:unit, :] = d0[...]
        down_ref[unit:, :] = d1[...]

    shapes = [jax.ShapeDtypeStruct((local, 4 * model), F32), jax.ShapeDtypeStruct((2 * unit, model), F32)]
    ins = (*mine, *theirs, *downs)
    return pl.pallas_call(
        kernel,
        grid=(1,),
        in_specs=[smem_spec(), *[whole(one.shape) for one in ins]],
        out_specs=[whole(one.shape) for one in shapes],
        out_shape=shapes,
        compiler_params=params(),
        name="finish_feed_forward",
    )(core, *ins)


VECTORS = 8


class GridLinks:
    pair = True

    def __init__(self, sizes, model):
        self.ny, self.nz, self.nx = sizes
        self.chips = self.ny * self.nz * self.nx
        self.rows = model // self.chips
        dp, inner = lax.axis_index("dp"), lax.axis_index("fsdp")
        self.core = inner % 2
        chip = inner // 2
        self.place = (dp, chip // self.nx, chip % self.nx)
        self.gather_offsets = [self._offsets(self.core ^ h, -1) for h in range(2)]
        self.scatter_offsets = self._offsets(self.core, 1)

    def _offsets(self, core, sign):
        y, z, x = self.place
        out = []
        for r1 in range(2):
            for r2 in range(2):
                for k in range(self.nz):
                    fy = jnp.where(core == 0, r1, r2)
                    fx = jnp.where(core == 0, r2, r1)
                    zz = (z + sign * k + self.nz) % self.nz
                    out.append(((y ^ fy) * self.nz + zz) * self.nx + (x ^ fx))
        return (jnp.stack(out) * self.rows).astype(jnp.int32)

    def _send(self, value, move):
        pairs = []
        for y in range(self.ny):
            for z in range(self.nz):
                for x in range(self.nx):
                    for c in range(2):
                        source = ((y * self.nz + z) * self.nx + x) * 2 + c
                        ty, tz, tx, tc = move(y, z, x, c)
                        pairs.append((source, ((ty * self.nz + tz) * self.nx + tx) * 2 + tc))
        return lax.ppermute(value, AXES, pairs)

    def swap(self, value):
        return self._send(value, lambda y, z, x, c: (y, z, x, 1 - c))

    def along_z(self, value, k):
        return self._send(value, lambda y, z, x, c: (y, (z + k) % self.nz, x, c))

    def x_first(self, value):
        return self._send(value, lambda y, z, x, c: (y, z, 1 - x, c) if c == 0 else (1 - y, z, x, c))

    def y_first(self, value):
        return self._send(value, lambda y, z, x, c: (y, z, 1 - x, c) if c == 1 else (1 - y, z, x, c))

    def gather(self, piece):
        parts = [piece] + [self.along_z(piece, k) for k in range(1, self.nz)]
        near = jnp.stack(parts)
        second = self.x_first(near)
        third = self.y_first(near)
        fourth = self.y_first(second)
        own = [near, second, third, fourth]
        other = [self.swap(one) for one in own]
        return (
            Pieces(own, self.gather_offsets[0], self.rows),
            Pieces(other, self.gather_offsets[1], self.rows),
        )

    def scatter(self, keep, send):
        n = self.nz

        def add(a, b):
            return (a.astype(F32) + b.astype(F32)).astype(BF)

        moved = self.y_first(send)
        send, keep = add(keep[n:], moved[n:]), add(keep[:n], moved[:n])
        moved = self.x_first(send)
        sums = [add(keep[k], moved[k]) for k in range(n)]
        return [sums[0]] + [self.along_z(sums[k], k) for k in range(1, n)]


def on_device(
    links,
    tokens,
    lengths,
    buckets,
    ln1_gain,
    ln1_bias,
    qkv_weight,
    q_bias,
    v_bias,
    out_weight,
    out_bias,
    rel_table,
    ln2_gain,
    ln2_bias,
    up_weight,
    up_bias,
    down_weight,
    down_bias,
    cotangent,
):
    rows, model = tokens.shape
    heads, number = rel_table.shape
    head_size = model // heads
    width = model // 2
    local = qkv_weight.shape[0]
    core, chips = links.core, links.chips
    core_arg = core.astype(jnp.int32).reshape(1)

    n_first = jnp.stack([ln1_gain, ln1_bias, q_bias, v_bias, out_bias, ln2_gain, ln2_bias, down_bias])
    spread = jnp.where(
        core == 0, jnp.pad(n_first, ((0, 0), (0, TILE - local))), jnp.pad(n_first, ((0, 0), (local, TILE - 2 * local)))
    )
    halves = jnp.pad(up_bias.reshape(2, 1, 2 * local), ((0, 0), (0, 0), (0, TILE - 2 * local)))
    blank = jnp.zeros_like(halves)
    halves = jnp.where(core == 0, jnp.concatenate([halves, blank], 1), jnp.concatenate([blank, halves], 1))
    small = jnp.concatenate([spread, halves.reshape(4, TILE), jnp.zeros((4, TILE), BF)], 0)
    small_theirs = links.swap(small)
    a_mine, a_sent, u_mine, u_sent = pack_blocks(core_arg, qkv_weight, out_weight, up_weight)
    a_theirs = links.swap(a_sent)
    u_theirs = links.swap(u_sent)
    a_piece = merge_attention(core_arg, a_mine, a_theirs, small, small_theirs)
    f_pieces = merge_feed_forward(core_arg, u_mine, u_theirs, down_weight)

    grad_rows = jnp.where(
        (jnp.arange(rows, dtype=jnp.int32) < lengths[0])[:, None], cotangent, jnp.zeros_like(cotangent)
    )
    grad_rows_other = links.swap(grad_rows)

    a_own, a_other = links.gather(a_piece)

    line = jnp.concatenate([buckets[0, rows - 1, :1], buckets[0, rows - 1, :], buckets[0, 0, 1:]])
    chosen = (jnp.arange(number, dtype=jnp.int32)[:, None] == line[None, :]).astype(BF)
    half_heads = heads // 2
    table_rel = jnp.where(
        core == 0, rel_table, jnp.concatenate([rel_table[half_heads:], rel_table[:half_heads]], 0)
    )
    curve = jnp.dot(table_rel, chosen, preferred_element_type=F32)
    tiles = bias_tiles(curve)

    normed, vec, joined0, mixed0, probs0 = attention_forward(
        0, core_arg, tokens, None, None, a_own, tiles, lengths, head_size
    )
    normed_other = links.swap(normed)
    joined1, mixed1, probs1 = attention_forward(
        1, core_arg, tokens, normed, vec, a_other, tiles, lengths, head_size
    )
    f_own, f_other = zip(*[links.gather(piece) for piece in f_pieces])
    residual, normed2 = project_out(core_arg, (mixed0, mixed1), tokens, (a_own, a_other), vec)
    normed2_other = links.swap(normed2)

    result, grad_n2 = residual, None
    up_sums, ffn = [], []
    for f in range(2):
        result, grad_n2, active, grad_pre, sums = feed_forward(
            f, core_arg, normed2, grad_rows, vec, (f_own[f], f_other[f]), result, grad_n2
        )
        up_sums.append(sums)
        active_other = links.swap(active[1])
        pre_other = links.swap(grad_pre[1])
        keep, send = outer_products(
            [
                ([(normed2, None), (normed2_other, None)], [(grad_pre, 0), (pre_other, None)]),
                ([(active, 0), (active_other, None)], [(grad_rows, None), (grad_rows_other, None)]),
            ],
            links.scatter_offsets,
            links.rows,
        )
        ffn.append(total_feed_forward(core_arg, links.scatter(keep, send), local))

    output, grad_res, grad_branch, gm0, gm1, sums2 = second_norm_back(
        core_arg, residual, result, grad_n2, grad_rows, (a_own, a_other), vec, lengths
    )
    branch_cols = lax.dynamic_slice_in_dim(grad_branch, core * width, width, 1)
    branch_theirs = lax.dynamic_slice_in_dim(grad_branch, (1 - core) * width, width, 1)
    branch_other = links.swap(branch_theirs)

    first = core == 0
    mixed = jnp.concatenate([jnp.where(first, mixed0, mixed1), jnp.where(first, mixed1, mixed0)], 1)
    mixed_other = links.swap(mixed)
    dj1, diag1 = attention_backward(joined1, probs1, mixed1, gm1, head_size)
    dj_other = links.swap(dj1)
    dj0, diag0 = attention_backward(joined0, probs0, mixed0, gm0, head_size)

    input_grad, vec_grads, table_grad = first_norm_back(
        core_arg, (dj0, dj1), tokens, grad_res, vec, (a_own, a_other), sums2, up_sums, (diag0, diag1), chosen
    )
    keep, send = outer_products(
        [([(normed, None), (normed_other, None)], [(dj0, j), (dj_other, j)]) for j in range(3)]
        + [([(mixed, None), (mixed_other, None)], [(branch_cols, None), (branch_other, None)])],
        links.scatter_offsets,
        links.rows,
        (vec_grads, table_grad),
    )
    mine, sent, tail = total_attention(core_arg, links.scatter(keep, send), local)
    theirs, tail_theirs = links.swap(sent), links.swap(tail)
    grad_qkv, grad_out, small, grad_table = finish_attention(
        core_arg, mine, theirs, tail, tail_theirs, heads, number
    )
    ups = [links.swap(one[1]) for one in ffn]
    grad_up, grad_down = finish_feed_forward(
        core_arg, [one[0] for one in ffn], ups, [one[2] for one in ffn]
    )
    small_grads = [small[i, :local] for i in range(VECTORS)]
    unit = 2 * local
    halves = small[8:12, :].reshape(2, 2, TILE)
    grad_up_bias = lax.dynamic_index_in_dim(halves, core, 1, keepdims=False)[:, :unit].reshape(2 * unit)

    return (
        output,
        input_grad,
        small_grads[0],
        small_grads[1],
        grad_qkv,
        small_grads[2],
        small_grads[3],
        grad_out,
        small_grads[4],
        grad_table,
        small_grads[5],
        small_grads[6],
        grad_up,
        grad_up_bias,
        grad_down,
        small_grads[7],
    )


def on_any_mesh(
    tokens,
    lengths,
    buckets,
    ln1_gain,
    ln1_bias,
    qkv_weight,
    q_bias,
    v_bias,
    out_weight,
    out_bias,
    rel_table,
    ln2_gain,
    ln2_bias,
    up_weight,
    up_bias,
    down_weight,
    down_bias,
    cotangent,
):
    rows, model = tokens.shape
    heads, number = rel_table.shape
    head_size = model // heads
    width = model // 2
    local = qkv_weight.shape[0]
    hidden = up_weight.shape[1]
    core = jnp.zeros((1,), jnp.int32)
    offsets = jnp.zeros((1,), jnp.int32)

    def gathered(x):
        return lax.all_gather(x, AXES, axis=0, tiled=True)

    def scattered(x):
        return lax.psum_scatter(x, AXES, scatter_dimension=0, tiled=True)

    vectors = [ln1_gain, ln1_bias, q_bias, v_bias, out_bias, ln2_gain, ln2_bias, down_bias]
    unit = up_bias.shape[0]
    small = gathered(jnp.concatenate([*vectors, up_bias])[None, :])
    wide = [small[:, i * local : (i + 1) * local].reshape(1, model) for i in range(VECTORS)]
    ub = small[:, VECTORS * local :].reshape(2, 2, model).transpose(1, 0, 2).reshape(4, model)
    del unit
    vec = jnp.concatenate([*wide, ub, jnp.zeros((4, model), BF)], 0).astype(F32)
    attn = gathered(jnp.concatenate([qkv_weight, out_weight], 1))
    up, down = gathered(up_weight), gathered(down_weight)
    a_pieces = tuple(
        Pieces(
            [jnp.concatenate([attn[:, j * model + h * width : j * model + (h + 1) * width] for j in range(4)], 0)[None]],
            offsets,
            model,
        )
        for h in range(2)
    )

    def chunk(f, h):
        at = (2 * h + f) * model
        return Pieces(
            [jnp.concatenate([up[:, at : at + model], down[at : at + model]], 0)[None]], offsets, model
        )

    grad_rows = jnp.where(
        (jnp.arange(rows, dtype=jnp.int32) < lengths[0])[:, None], cotangent, jnp.zeros_like(cotangent)
    )
    line = jnp.concatenate([buckets[0, rows - 1, :1], buckets[0, rows - 1, :], buckets[0, 0, 1:]])
    chosen = (jnp.arange(number, dtype=jnp.int32)[:, None] == line[None, :]).astype(BF)
    tiles = bias_tiles(jnp.dot(rel_table, chosen, preferred_element_type=F32))
    normed, joined0, mixed0, probs0 = attention_forward(
        0, core, tokens, None, vec, a_pieces[0], tiles, lengths, head_size
    )
    joined1, mixed1, probs1 = attention_forward(
        1, core, tokens, normed, vec, a_pieces[1], tiles, lengths, head_size
    )
    residual, normed2 = project_out(core, (mixed0, mixed1), tokens, a_pieces, vec)
    result, grad_n2 = residual, None
    up_sums, ups, downs = [], [], []
    for f in range(2):
        result, grad_n2, active, grad_pre, sums = feed_forward(
            f, core, normed2, grad_rows, vec, (chunk(f, 0), chunk(f, 1)), result, grad_n2
        )
        up_sums.append(sums)
        for h in range(2):
            (both,) = outer_products(
                [([(normed2, None)], [(grad_pre, h)]), ([(active, h)], [(grad_rows, None)])], offsets, model
            )
            ups.append(both[0, :model])
            downs.append(both[0, model:])
    output, grad_res, grad_branch, gm0, gm1, sums2 = second_norm_back(
        core, residual, result, grad_n2, grad_rows, a_pieces, vec, lengths
    )
    dj0, diag0 = attention_backward(joined0, probs0, mixed0, gm0, head_size)
    dj1, diag1 = attention_backward(joined1, probs1, mixed1, gm1, head_size)
    input_grad, vec_grads, table_grad = first_norm_back(
        core, (dj0, dj1), tokens, grad_res, vec, a_pieces, sums2, up_sums, (diag0, diag1), chosen
    )
    mixed = jnp.concatenate([mixed0, mixed1], 1)
    halves = [
        outer_products(
            [([(normed, None)], [(dj, j)]) for j in range(3)]
            + [([(mixed, None)], [(grad_branch[:, h * width : (h + 1) * width], None)])],
            offsets,
            model,
        )[0][0].reshape(4, model, width)
        for h, dj in enumerate((dj0, dj1))
    ]
    grads = jnp.stack(halves, 2).transpose(1, 0, 2, 3).reshape(model, 4 * model)
    grads = scattered(grads)
    grad_up = scattered(jnp.concatenate([ups[0], ups[2], ups[1], ups[3]], 1))
    grad_down = scattered(jnp.concatenate([downs[0], downs[2], downs[1], downs[3]], 0))
    by_owner = vec_grads[:VECTORS].reshape(VECTORS, model // local, local).transpose(1, 0, 2)
    own_units = vec_grads[VECTORS : VECTORS + 4].reshape(2, 2, model).transpose(1, 0, 2)
    both = jnp.concatenate(
        [by_owner.reshape(model // local, VECTORS * local), own_units.reshape(model // local, hidden * local // model)],
        1,
    )
    both = scattered(both)[0]
    table = jnp.concatenate([table_grad[16:], table_grad[:16, TILE : TILE + number - width]], 1)[:heads]
    grad_table = lax.psum(table, AXES)
    small_grads = [both[i * local : (i + 1) * local] for i in range(VECTORS)]
    return (
        output,
        input_grad,
        small_grads[0],
        small_grads[1],
        grads[:, : 3 * model].astype(F32),
        small_grads[2],
        small_grads[3],
        grads[:, 3 * model :].astype(F32),
        small_grads[4],
        grad_table,
        small_grads[5],
        small_grads[6],
        grad_up.astype(F32),
        both[VECTORS * local :],
        grad_down.astype(F32),
        small_grads[7],
    )


def solution(mesh):
    both = P(AXES)
    row = P(AXES, None)
    in_specs = (
        row, both, P(AXES, None, None), both, both, row, both, both, row, both, P(), both, both, row, both, row,
        both, row,
    )
    out_specs = (row, row, both, both, row, both, both, row, both, P(), both, both, row, both, row, both)

    if tuple(mesh.shape[name] for name in AXES) == (2, 16):

        def body(*args):
            return on_device(GridLinks((2, 4, 2), args[0].shape[1]), *args)

    else:
        body = on_any_mesh

    return jax.shard_map(body, mesh=mesh, in_specs=in_specs, out_specs=out_specs, check_vma=False)
```

time: 1600 us -> 322 us (0.20)
  local copies, waits for them, and re-layouts: 1010 us -> 20.3 us
  matrix products: 204 us -> 0.42 us
  waiting for transfers between devices: 247 us -> 79.5 us
  Pallas kernels: 0 us -> 124 us
  blocking collectives: 85.1 us -> 0 us
  starting transfers between devices: 0.32 us -> 80.9 us
  other arithmetic: 28.6 us -> 10.2 us
    gather x2 -> x0, local copies, waits for them, and re-layouts: 934 us -> none  [forward_item(): table_float[:, bucket]]
    reduce_scatter x4 -> x0, waiting for transfers between devices: 244 us -> none  [the longest x1 142 us: on_device(): lax.psum_scatter(grad_down, ('dp', 'fsdp'), scatter_dimension=0, tiled=True)]
    dot_general x26 -> x1, matrix products: 204 us -> 0.42 us  [on_device(): curve = jnp.dot(table_rel, chosen, preferred_element_type=F32)]
    pallas_call x0 -> x21, Pallas kernels: none -> 124 us  [the longest x2 24.2 us: feed_forward(): pl.pallas_call(kernel, grid=(2,), in_specs=specs + [any_spec()] * (sum(si...]
    unnamed x2 -> x0, blocking collectives: 85.1 us -> none
    ppermute x0 -> x62, starting transfers between devices: none -> 80.9 us  [_send(): return lax.ppermute(value, AXES, pairs)]
    ppermute x0 -> x62, waiting for transfers between devices: none -> 79.5 us  [_send(): return lax.ppermute(value, AXES, pairs)]
    unnamed x77 -> x110, local copies, waits for them, and re-layouts: 33.7 us -> 9.18 us
  transfers between devices with their start and end apart: 8 -> 62, of which waited for: 2 -> 13; matrix products, arithmetic and copies ran while one was open for 76% -> 6% of each run, Pallas kernels for 0% -> 37%
where the time goes in v1:
time: 322 us; the launch traced here: 317 us
  Pallas kernels  124 us (39%)
  starting transfers between devices  80.9 us (25%)
  waiting for transfers between devices  79.5 us (25%)
  local copies, waits for them, and re-layouts  20.3 us (6%)
  other arithmetic  10.2 us (3%)
    ppermute x62, starting transfers between devices, _send(): return lax.ppermute(value, AXES, pairs)  80.9 us
    ppermute x62, waiting for transfers between devices, _send(): return lax.ppermute(value, AXES, pairs)  79.5 us
    pallas_call x2, Pallas kernels, feed_forward(): pl.pallas_call(kernel, grid=(2,), in_specs=specs + [any_spec()] * (sum(si...  24.2 us
    pallas_call x3, Pallas kernels, outer_products(): pl.pallas_call(kernel, grid=(1,), in_specs=specs, out_specs=[any_spec()]...  22.6 us
    pallas_call x2, Pallas kernels, attention_forward(): pl.pallas_call(kernel, grid=(pairs,), in_specs=specs, out_specs=outs, out...  19.9 us
    pallas_call x2, Pallas kernels, attention_backward(): pl.pallas_call(kernel, grid=(pairs,), in_specs=[pl.BlockSpec((3, rows, TI...  12.9 us
    pallas_call x1, Pallas kernels, first_norm_back(): pl.pallas_call(kernel, grid=(1,), in_specs=[*[smem_spec()] * 3, whole((3,...  10 us
    unnamed x110, local copies, waits for them, and re-layouts  9.18 us
  transfers between devices with their start and end apart: 62, of which 13 were waited for; matrix products, arithmetic and copies ran while one was open for 6% of the time, Pallas kernels for 37%

profile of v1, /device:TPU:0, one launch (start us, length us, event | category | flops | bytes accessed | tf_op | source)
XLA Modules:
  0.0 317.3 jit_solution(7311860488660141235)
XLA Ops:
  28.2 9.4 %collective-permute-done.14 = bf16[96,768]{1,0:T(8,128)(2,1)S(1)} collective-permute-done((bf16[96,768]{1,0:T(8,128)(2,1)}, bf16[96,768]{1,0:T(8,128)(2,1)S(1)}, u32[]{:S(2)}, u32[]{:S(2)}) %collective-permute-start.14) | collective-permute-done | bytes 147488 | tf_op jit(solution)/shard_map/ppermute | solution.py:1049
  40.3 3.7 %collective-permute-start.23 = (bf16[96,768]{1,0:T(8,128)(2,1)S(1)}, bf16[96,768]{1,0:T(8,128)(2,1)S(1)}, u32[]{:S(2)}, u32[]{:S(2)}) collective-permute-start(bf16[96,768]{1,0:T(8,128)(2,1)S(1)} %copy-done.25), channel_id=1, source_target_pairs={{0,4},{1,5},{2,6},{3,7},{4,8},{5,9},{6,10},{7,11},{8,12},{9,13},{1... | collective-permute-start | bytes 442376 | tf_op jit(solution)/shard_map/ppermute | solution.py:1049
  64.2 8.9 %collective-permute-done.6.refs_3_.rest_2_ = bf16[4,208,384]{2,1,0:T(8,128)(2,1)S(1)} collective-permute-done((bf16[4,208,384]{2,1,0:T(8,128)(2,1)S(1)}, bf16[4,208,384]{2,1,0:T(8,128)(2,1)S(1)}, u32[]{:S(2)}, u32[]{:S(2)}) %collective-permute-start.6) | collective-permute-done | bytes 639008 | tf_op jit(solution)/shard_map/ppermute | solution.py:1049
  73.2 6.8 %collective-permute-done.7.refs_4_.rest_3_ = bf16[4,208,384]{2,1,0:T(8,128)(2,1)S(1)} collective-permute-done((bf16[4,208,384]{2,1,0:T(8,128)(2,1)S(1)}, bf16[4,208,384]{2,1,0:T(8,128)(2,1)S(1)}, u32[]{:S(2)}, u32[]{:S(2)}) %collective-permute-start.7) | collective-permute-done | bytes 639008 | tf_op jit(solution)/shard_map/ppermute | solution.py:1049
  81.2 7.5 %bias_tiles.1.refs_0_.refs_1_ = bf16[12,7,128,128]{3,2,1,0:T(8,128)(2,1)} custom-call(f32[12,1,1024]{2,1,0:T(1,128)} %reshape.104.curve_ref), custom_call_target="tpu_custom_call" | custom-call | tf_op jit(solution)/shard_map/bias_tiles/pallas_call | solution.py:97
  93.0 6.6 %collective-permute-done.18.rest_3_ = bf16[4,96,768]{2,1,0:T(8,128)(2,1)S(1)} collective-permute-done((bf16[4,96,768]{2,1,0:T(8,128)(2,1)}, bf16[4,96,768]{2,1,0:T(8,128)(2,1)S(1)}, u32[]{:S(2)}, u32[]{:S(2)}) %collective-permute-start.18) | collective-permute-done | bytes 589856 | tf_op jit(solution)/shard_map/ppermute | solution.py:1049
  101.7 10.0 %attention_forward.2 = (bf16[512,768]{1,0:T(8,128)(2,1)}, f32[16,768]{1,0:T(8,128)}, bf16[3,512,384]{2,1,0:T(8,128)(2,1)}, bf16[512,384]{1,0:T(8,128)(2,1)}, bf16[6,512,512]{2,1,0:T(8,128)(2,1)}) custom-call(s32[1]{0:T(128)} %bitcast.core_ref, s32[16]{0:T(128)} %broadcast_multiply_fusion.2.offs_ref.offs0, s32[1]{0:T(128)} %copy.35.len_ref, ...), custom_call_target="tpu_custom_call" | custom-call | flops 2000000000 | bytes 10000000 | tf_op jit(solution)/shard_map/attention_forward/pallas_call | solution.py:235
  111.7 9.8 %attention_forward.3 = (bf16[3,512,384]{2,1,0:T(8,128)(2,1)}, bf16[512,384]{1,0:T(8,128)(2,1)}, bf16[6,512,512]{2,1,0:T(8,128)(2,1)}) custom-call(s32[1]{0:T(128)} %bitcast.core_ref, s32[16]{0:T(128)} %broadcast_multiply_fusion.1.offs_ref.offs1, s32[1]{0:T(128)} %copy.35.len_ref, bf16[512,768]{1,0:T(8,128)(2,1)} %get-tuple-element.79.x_ref.rest_0_, ...), custom_call_target="tpu_custom_call" | custom-call | flops 2000000000 | bytes 10000000 | tf_op jit(solution)/shard_map/attention_forward/pallas_call | solution.py:235
  121.6 5.5 %project_out.1 = (f32[512,768]{1,0:T(8,128)}, bf16[512,768]{1,0:T(8,128)(2,1)}) custom-call(s32[1]{0:T(128)} %bitcast.core_ref, s32[16]{0:T(128)} %broadcast_multiply_fusion.2.offs_ref.offs0, s32[16]{0:T(128)} %broadcast_multiply_fusion.1.offs_ref.offs1, bf16[512,384]{1,0:T(8,128)(2,1)} %get-tuple-element.78.m0_ref.mixed_ref, ...), custom_call_target="tpu_custom_call" | custom-call | flops 600000000 | bytes 5000000 | tf_op jit(solution)/shard_map/project_out/pallas_call | solution.py:284
  129.3 12.0 %feed_forward.2 = (f32[512,768]{1,0:T(8,128)}, f32[512,768]{1,0:T(8,128)}, bf16[2,512,768]{2,1,0:T(8,128)(2,1)}, bf16[2,512,768]{2,1,0:T(8,128)(2,1)}, f32[2,1,768]{2,1,0:T(1,128)}) custom-call(s32[1]{0:T(128)} %bitcast.core_ref, s32[16]{0:T(128)} %broadcast_multiply_fusion.2.offs_ref.offs0, s32[16]{0:T(128)} %broadcast_multiply_fusion.1.offs_ref.offs1, ...), custom_call_target="tpu_custom_call" | custom-call | flops 6400000000 | bytes 20000000 | tf_op jit(solution)/shard_map/feed_forward/pallas_call | solution.py:378
  142.6 12.2 %feed_forward.3 = (f32[512,768]{1,0:T(8,128)}, f32[512,768]{1,0:T(8,128)}, bf16[2,512,768]{2,1,0:T(8,128)(2,1)}, bf16[2,512,768]{2,1,0:T(8,128)(2,1)}, f32[2,1,768]{2,1,0:T(1,128)}) custom-call(s32[1]{0:T(128)} %bitcast.core_ref, s32[16]{0:T(128)} %broadcast_multiply_fusion.2.offs_ref.offs0, s32[16]{0:T(128)} %broadcast_multiply_fusion.1.offs_ref.offs1, ...), custom_call_target="tpu_custom_call" | custom-call | flops 6400000000 | bytes 20000000 | tf_op jit(solution)/shard_map/feed_forward/pallas_call | solution.py:378
  157.1 6.5 %second_norm_back.1 = (bf16[512,768]{1,0:T(8,128)(2,1)}, f32[512,768]{1,0:T(8,128)}, bf16[512,768]{1,0:T(8,128)(2,1)}, bf16[512,384]{1,0:T(8,128)(2,1)}, bf16[512,384]{1,0:T(8,128)(2,1)}, /*index=5*/f32[8,768]{1,0:T(8,128)}) custom-call(s32[1]{0:T(128)} %bitcast.core_ref, s32[1]{0:T(128)} %copy.35.len_ref, s32[16]{0:T(128)} %broadcast_multiply_fusion.2.offs_ref.offs0, ...), custom_call_target="tpu_custom_call" | custom-call | flops 600000000 | bytes 10000000 | tf_op jit(solution)/shard_map/second_norm_back/pallas_call | solution.py:557
  163.5 6.2 %attention_backward.3 = (bf16[3,512,384]{2,1,0:T(8,128)(2,1)}, f32[6,1,1024]{2,1,0:T(1,128)}) custom-call(bf16[3,512,384]{2,1,0:T(8,128)(2,1)} %get-tuple-element.97.joined_ref, bf16[6,512,512]{2,1,0:T(8,128)(2,1)} %get-tuple-element.98.p_ref, bf16[512,384]{1,0:T(8,128)(2,1)} %get-tuple-element.81.m1_ref.mixed_ref, bf16[512,384]{1,0:T(8,128)(2,1)} %get-tuple-element.99.gm_ref), custom_call_target="tpu_custom_call" | custom-call | flops 4000000000 | bytes 10000000 | tf_op jit(solution)/shard_map/attention_backward/pallas_call | solution.py:641
  170.1 6.7 %attention_backward.2 = (bf16[3,512,384]{2,1,0:T(8,128)(2,1)}, f32[6,1,1024]{2,1,0:T(1,128)}) custom-call(bf16[3,512,384]{2,1,0:T(8,128)(2,1)} %get-tuple-element.93.joined_ref, bf16[6,512,512]{2,1,0:T(8,128)(2,1)} %get-tuple-element.94.p_ref, bf16[512,384]{1,0:T(8,128)(2,1)} %get-tuple-element.78.m0_ref.mixed_ref, bf16[512,384]{1,0:T(8,128)(2,1)} %get-tuple-element.95.gm_ref), custom_call_target="tpu_custom_call" | custom-call | flops 4000000000 | bytes 10000000 | tf_op jit(solution)/shard_map/attention_backward/pallas_call | solution.py:641
  181.3 10.0 %first_norm_back.1 = (f32[512,768]{1,0:T(8,128)}, f32[16,768]{1,0:T(8,128)}, f32[32,384]{1,0:T(8,128)}) custom-call(s32[1]{0:T(128)} %bitcast.core_ref, s32[16]{0:T(128)} %broadcast_multiply_fusion.2.offs_ref.offs0, s32[16]{0:T(128)} %broadcast_multiply_fusion.1.offs_ref.offs1, bf16[3,512,384]{2,1,0:T(8,128)(2,1)} %get-tuple-element.96.d0_ref.rest_2_, ...), custom_call_target="tpu_custom_call" | custom-call | flops 2000000000 | bytes 10000000 | tf_op jit(solution)/shard_map/first_norm_back/pallas_call | solution.py:743
  191.4 7.3 %outer_products.5 = (bf16[8,96,768]{2,1,0:T(8,128)(2,1)}, bf16[8,96,768]{2,1,0:T(8,128)(2,1)}) custom-call(s32[16]{0:T(128)} %broadcast_multiply_fusion.offs_ref, bf16[512,768]{1,0:T(8,128)(2,1)} %get-tuple-element.83.n_ref.rest_0_, bf16[512,768]{1,0:T(8,128)(2,1)} %copy-done.11, bf16[2,512,768]{2,1,0:T(8,128)(2,1)} %get-tuple-element.125.rest_2_, ...), custom_call_target="tpu_custom_call" | custom-call | flops 2000000000 | bytes 10000000 | tf_op jit(solution)/shard_map/outer_products/pallas_call | solution.py:489
  200.6 7.9 %outer_products.3 = (bf16[8,224,384]{2,1,0:T(8,128)(2,1)}, bf16[8,224,384]{2,1,0:T(8,128)(2,1)}) custom-call(s32[16]{0:T(128)} %broadcast_multiply_fusion.offs_ref, bf16[512,768]{1,0:T(8,128)(2,1)} %get-tuple-element.79.x_ref.rest_0_, bf16[512,768]{1,0:T(8,128)(2,1)} %collective-permute-done.33.rest_1_, ...), custom_call_target="tpu_custom_call" | custom-call | flops 2000000000 | bytes 10000000 | tf_op jit(solution)/shard_map/outer_products/pallas_call | solution.py:489
  211.0 7.3 %outer_products.4 = (bf16[8,96,768]{2,1,0:T(8,128)(2,1)}, bf16[8,96,768]{2,1,0:T(8,128)(2,1)}) custom-call(s32[16]{0:T(128)} %broadcast_multiply_fusion.offs_ref, bf16[512,768]{1,0:T(8,128)(2,1)} %get-tuple-element.83.n_ref.rest_0_, bf16[512,768]{1,0:T(8,128)(2,1)} %copy-done.11, bf16[2,512,768]{2,1,0:T(8,128)(2,1)} %get-tuple-element.120.rest_2_, ...), custom_call_target="tpu_custom_call" | custom-call | flops 2000000000 | bytes 10000000 | tf_op jit(solution)/shard_map/outer_products/pallas_call | solution.py:489
  220.4 15.9 %collective-permute-done.37 = bf16[8,224,384]{2,1,0:T(8,128)(2,1)S(1)} collective-permute-done((bf16[8,224,384]{2,1,0:T(8,128)(2,1)}, bf16[8,224,384]{2,1,0:T(8,128)(2,1)S(1)}, u32[]{:S(2)}, u32[]{:S(2)}) %collective-permute-start.37) | collective-permute-done | bytes 1376288 | tf_op jit(solution)/shard_map/ppermute | solution.py:1049
  237.3 19.1 %collective-permute-done.48 = bf16[8,96,768]{2,1,0:T(8,128)(2,1)S(1)} collective-permute-done((bf16[8,96,768]{2,1,0:T(8,128)(2,1)}, bf16[8,96,768]{2,1,0:T(8,128)(2,1)S(1)}, u32[]{:S(2)}, u32[]{:S(2)}) %collective-permute-start.48) | collective-permute-done | bytes 1179680 | tf_op jit(solution)/shard_map/ppermute | solution.py:1049
  258.0 3.8 %collective-permute-start.57 = (bf16[96,768]{1,0:T(8,128)(2,1)S(1)}, bf16[96,768]{1,0:T(8,128)(2,1)S(1)}, u32[]{:S(2)}, u32[]{:S(2)}) collective-permute-start(bf16[96,768]{1,0:T(8,128)(2,1)S(1)} %get-tuple-element.148), channel_id=1, source_target_pairs={{0,4},{1,5},{2,6},{3,7},{4,8},{5,9},{6,10},{7,11},{8,12},{9,13},{1... | collective-permute-start | bytes 442376 | tf_op jit(solution)/shard_map/ppermute | solution.py:1049
  270.0 5.0 %collective-permute-start.59 = (bf16[96,768]{1,0:T(8,128)(2,1)S(1)}, bf16[96,768]{1,0:T(8,128)(2,1)S(1)}, u32[]{:S(2)}, u32[]{:S(2)}) collective-permute-start(bf16[96,768]{1,0:T(8,128)(2,1)S(1)} %get-tuple-element.146), channel_id=1, source_target_pairs={{0,12},{1,13},{2,14},{3,15},{4,0},{5,1},{6,2},{7,3},{8,4},{9,5},{1... | collective-permute-start | bytes 442376 | tf_op jit(solution)/shard_map/ppermute | solution.py:1049
  275.0 13.7 %collective-permute-start.50 = (bf16[96,768]{1,0:T(8,128)(2,1)S(1)}, bf16[96,768]{1,0:T(8,128)(2,1)S(1)}, u32[]{:S(2)}, u32[]{:S(2)}) collective-permute-start(bf16[96,768]{1,0:T(8,128)(2,1)S(1)} %get-tuple-element.152), channel_id=1, source_target_pairs={{0,4},{1,5},{2,6},{3,7},{4,8},{5,9},{6,10},{7,11},{8,12},{9,13},{1... | collective-permute-start | bytes 442376 | tf_op jit(solution)/shard_map/ppermute | solution.py:1049
  290.7 9.3 %collective-permute-start.52 = (bf16[96,768]{1,0:T(8,128)(2,1)S(1)}, bf16[96,768]{1,0:T(8,128)(2,1)S(1)}, u32[]{:S(2)}, u32[]{:S(2)}) collective-permute-start(bf16[96,768]{1,0:T(8,128)(2,1)S(1)} %get-tuple-element.150), channel_id=1, source_target_pairs={{0,12},{1,13},{2,14},{3,15},{4,0},{5,1},{6,2},{7,3},{8,4},{9,5},{1... | collective-permute-start | bytes 442376 | tf_op jit(solution)/shard_map/ppermute | solution.py:1049
  (276 shorter events, 103.7 us)
Async XLA Ops:
  26.1 29.4 %collective-permute-start.5 = (bf16[4,208,384]{2,1,0:T(8,128)(2,1)S(1)}, bf16[4,208,384]{2,1,0:T(8,128)(2,1)S(1)}, u32[]{:S(2)}, u32[]{:S(2)}) collective-permute-start(bf16[4,208,384]{2,1,0:T(8,128)(2,1)S(1)} %pad_maximum_fusion.1.refs_1_.rest_0_), channel_id=1, source_target_pairs={{0,2},{1,17},{2,0},{3,19},{4,6},{5,21},{6,4},{7,23},{8,10},{9,25},... | collective-permute-start | bytes 1916936 | tf_op jit(solution)/shard_map/ppermute | solution.py:1049
  55.5 24.6 %collective-permute-start.7 = (bf16[4,208,384]{2,1,0:T(8,128)(2,1)S(1)}, bf16[4,208,384]{2,1,0:T(8,128)(2,1)S(1)}, u32[]{:S(2)}, u32[]{:S(2)}) collective-permute-start(bf16[4,208,384]{2,1,0:T(8,128)(2,1)S(1)} %collective-permute-done.5.refs_2_.rest_1_), channel_id=1, source_target_pairs={{0,16},{1,3},{2,18},{3,1},{4,20},{5,7},{6,22},{7,5},{8,24},{9,11},... | collective-permute-start | bytes 1916936 | tf_op jit(solution)/shard_map/ppermute | solution.py:1049
  57.7 31.7 %collective-permute-start.26 = (bf16[4,96,768]{2,1,0:T(8,128)(2,1)}, bf16[4,96,768]{2,1,0:T(8,128)(2,1)}, u32[]{:S(2)}, u32[]{:S(2)}) collective-permute-start(bf16[4,96,768]{2,1,0:T(8,128)(2,1)} %pad_maximum_fusion.3.rest_1_), channel_id=1, source_target_pairs={{0,2},{1,17},{2,0},{3,19},{4,6},{5,21},{6,4},{7,23},{8,10},{9,25},... | collective-permute-start | bytes 1769480 | tf_op jit(solution)/shard_map/ppermute | solution.py:1049
  63.6 28.7 %collective-permute-start.8 = (bf16[4,208,384]{2,1,0:T(8,128)(2,1)S(1)}, bf16[4,208,384]{2,1,0:T(8,128)(2,1)S(1)}, u32[]{:S(2)}, u32[]{:S(2)}) collective-permute-start(bf16[4,208,384]{2,1,0:T(8,128)(2,1)S(1)} %pad_maximum_fusion.1.refs_1_.rest_0_), channel_id=1, source_target_pairs={{0,1},{1,0},{2,3},{3,2},{4,5},{5,4},{6,7},{7,6},{8,9},{9,8},{10,11... | collective-permute-start | bytes 1916936 | tf_op jit(solution)/shard_map/ppermute | solution.py:1049
  63.7 36.4 %collective-permute-start.9 = (bf16[4,208,384]{2,1,0:T(8,128)(2,1)S(1)}, bf16[4,208,384]{2,1,0:T(8,128)(2,1)}, u32[]{:S(2)}, u32[]{:S(2)}) collective-permute-start(bf16[4,208,384]{2,1,0:T(8,128)(2,1)S(1)} %collective-permute-done.5.refs_2_.rest_1_), channel_id=1, source_target_pairs={{0,1},{1,0},{2,3},{3,2},{4,5},{5,4},{6,7},{7,6},{8,9},{9,8},{10,11... | collective-permute-start | bytes 1916936 | tf_op jit(solution)/shard_map/ppermute | solution.py:1049
  73.2 26.4 %collective-permute-start.10 = (bf16[4,208,384]{2,1,0:T(8,128)(2,1)S(1)}, bf16[4,208,384]{2,1,0:T(8,128)(2,1)}, u32[]{:S(2)}, u32[]{:S(2)}) collective-permute-start(bf16[4,208,384]{2,1,0:T(8,128)(2,1)S(1)} %collective-permute-done.6.refs_3_.rest_2_), channel_id=1, source_target_pairs={{0,1},{1,0},{2,3},{3,2},{4,5},{5,4},{6,7},{7,6},{8,9},{9,8},{10,11... | collective-permute-start | bytes 1916936 | tf_op jit(solution)/shard_map/ppermute | solution.py:1049
  92.4 34.8 %collective-permute-start.27 = (bf16[4,96,768]{2,1,0:T(8,128)(2,1)}, bf16[4,96,768]{2,1,0:T(8,128)(2,1)S(1)}, u32[]{:S(2)}, u32[]{:S(2)}) collective-permute-start(bf16[4,96,768]{2,1,0:T(8,128)(2,1)} %pad_maximum_fusion.3.rest_1_), channel_id=1, source_target_pairs={{0,16},{1,3},{2,18},{3,1},{4,20},{5,7},{6,22},{7,5},{8,24},{9,11},... | collective-permute-start | bytes 1769480 | tf_op jit(solution)/shard_map/ppermute | solution.py:1049
  99.6 28.2 %collective-permute-start.20 = (bf16[4,96,768]{2,1,0:T(8,128)(2,1)S(1)}, bf16[4,96,768]{2,1,0:T(8,128)(2,1)S(1)}, u32[]{:S(2)}, u32[]{:S(2)}) collective-permute-start(bf16[4,96,768]{2,1,0:T(8,128)(2,1)S(1)} %copy-done.46), channel_id=1, source_target_pairs={{0,1},{1,0},{2,3},{3,2},{4,5},{5,4},{6,7},{7,6},{8,9},{9,8},{10,11... | collective-permute-start | bytes 1769480 | tf_op jit(solution)/shard_map/ppermute | solution.py:1049
  99.6 28.2 %collective-permute-start.21 = (bf16[4,96,768]{2,1,0:T(8,128)(2,1)}, bf16[4,96,768]{2,1,0:T(8,128)(2,1)}, u32[]{:S(2)}, u32[]{:S(2)}) collective-permute-start(bf16[4,96,768]{2,1,0:T(8,128)(2,1)} %collective-permute-done.17.rest_2_), channel_id=1, source_target_pairs={{0,1},{1,0},{2,3},{3,2},{4,5},{5,4},{6,7},{7,6},{8,9},{9,8},{10,11... | collective-permute-start | bytes 1769480 | tf_op jit(solution)/shard_map/ppermute | solution.py:1049
  100.1 28.2 %collective-permute-start.28 = (bf16[4,96,768]{2,1,0:T(8,128)(2,1)}, bf16[4,96,768]{2,1,0:T(8,128)(2,1)S(1)}, u32[]{:S(2)}, u32[]{:S(2)}) collective-permute-start(bf16[4,96,768]{2,1,0:T(8,128)(2,1)} %collective-permute-done.26.rest_2_), channel_id=1, source_target_pairs={{0,16},{1,3},{2,18},{3,1},{4,20},{5,7},{6,22},{7,5},{8,24},{9,11},... | collective-permute-start | bytes 1769480 | tf_op jit(solution)/shard_map/ppermute | solution.py:1049
  101.7 26.7 %collective-permute-start.22 = (bf16[4,96,768]{2,1,0:T(8,128)(2,1)S(1)}, bf16[4,96,768]{2,1,0:T(8,128)(2,1)S(1)}, u32[]{:S(2)}, u32[]{:S(2)}) collective-permute-start(bf16[4,96,768]{2,1,0:T(8,128)(2,1)S(1)} %collective-permute-done.18.rest_3_), channel_id=1, source_target_pairs={{0,1},{1,0},{2,3},{3,2},{4,5},{5,4},{6,7},{7,6},{8,9},{9,8},{10,11... | collective-permute-start | bytes 1769480 | tf_op jit(solution)/shard_map/ppermute | solution.py:1049
  127.2 49.7 %collective-permute-start.47 = (bf16[512,768]{1,0:T(8,128)(2,1)S(1)}, bf16[512,768]{1,0:T(8,128)(2,1)S(1)}, u32[]{:S(2)}, u32[]{:S(2)}) collective-permute-start(bf16[512,768]{1,0:T(8,128)(2,1)S(1)} %broadcast_select_fusion.gr_ref.rest_6_), channel_id=1, source_target_pairs={{0,1},{1,0},{2,3},{3,2},{4,5},{5,4},{6,7},{7,6},{8,9},{9,8},{10,11... | collective-permute-start | bytes 2359304 | tf_op jit(solution)/shard_map/ppermute | solution.py:1049
  141.4 35.8 %collective-permute-start.33 = (bf16[512,768]{1,0:T(8,128)(2,1)S(1)}, bf16[512,768]{1,0:T(8,128)(2,1)}, u32[]{:S(2)}, u32[]{:S(2)}) collective-permute-start(bf16[512,768]{1,0:T(8,128)(2,1)S(1)} %copy-done.43), channel_id=1, source_target_pairs={{0,1},{1,0},{2,3},{3,2},{4,5},{5,4},{6,7},{7,6},{8,9},{9,8},{10,11... | collective-permute-start | bytes 2359304 | tf_op jit(solution)/shard_map/ppermute | solution.py:1049
  141.8 38.9 %collective-permute-start.44 = (bf16[512,768]{1,0:T(8,128)(2,1)S(1)}, bf16[512,768]{1,0:T(8,128)(2,1)S(1)}, u32[]{:S(2)}, u32[]{:S(2)}) collective-permute-start(bf16[512,768]{1,0:T(8,128)(2,1)S(1)} %copy-done.9), channel_id=1, source_target_pairs={{0,1},{1,0},{2,3},{3,2},{4,5},{5,4},{6,7},{7,6},{8,9},{9,8},{10,11... | collective-permute-start | bytes 2359304 | tf_op jit(solution)/shard_map/ppermute | solution.py:1049
  169.8 29.6 %collective-permute-start.34 = (bf16[3,512,384]{2,1,0:T(8,128)(2,1)}, bf16[3,512,384]{2,1,0:T(8,128)(2,1)S(1)}, u32[]{:S(2)}, u32[]{:S(2)}) collective-permute-start(bf16[3,512,384]{2,1,0:T(8,128)(2,1)} %get-tuple-element.100.d1_ref), channel_id=1, source_target_pairs={{0,1},{1,0},{2,3},{3,2},{4,5},{5,4},{6,7},{7,6},{8,9},{9,8},{10,11... | collective-permute-start | bytes 3538952 | tf_op jit(solution)/shard_map/ppermute | solution.py:1049
  180.5 29.6 %collective-permute-start.45 = (bf16[512,768]{1,0:T(8,128)(2,1)S(1)}, bf16[512,768]{1,0:T(8,128)(2,1)}, u32[]{:S(2)}, u32[]{:S(2)}) collective-permute-start(bf16[512,768]{1,0:T(8,128)(2,1)S(1)} %slice_bitcast_fusion.3), channel_id=1, source_target_pairs={{0,1},{1,0},{2,3},{3,2},{4,5},{5,4},{6,7},{7,6},{8,9},{9,8},{10,11... | collective-permute-start | bytes 2359304 | tf_op jit(solution)/shard_map/ppermute | solution.py:1049
  180.7 29.4 %collective-permute-start.46 = (bf16[512,768]{1,0:T(8,128)(2,1)S(1)}, bf16[512,768]{1,0:T(8,128)(2,1)S(1)}, u32[]{:S(2)}, u32[]{:S(2)}) collective-permute-start(bf16[512,768]{1,0:T(8,128)(2,1)S(1)} %slice_bitcast_fusion.2), channel_id=1, source_target_pairs={{0,1},{1,0},{2,3},{3,2},{4,5},{5,4},{6,7},{7,6},{8,9},{9,8},{10,11... | collective-permute-start | bytes 2359304 | tf_op jit(solution)/shard_map/ppermute | solution.py:1049
  208.5 27.8 %collective-permute-start.37 = (bf16[8,224,384]{2,1,0:T(8,128)(2,1)}, bf16[8,224,384]{2,1,0:T(8,128)(2,1)S(1)}, u32[]{:S(2)}, u32[]{:S(2)}) collective-permute-start(bf16[8,224,384]{2,1,0:T(8,128)(2,1)} %get-tuple-element.112), channel_id=1, source_target_pairs={{0,16},{1,3},{2,18},{3,1},{4,20},{5,7},{6,22},{7,5},{8,24},{9,11},... | collective-permute-start | bytes 4128776 | tf_op jit(solution)/shard_map/ppermute | solution.py:1049
  218.3 38.0 %collective-permute-start.48 = (bf16[8,96,768]{2,1,0:T(8,128)(2,1)}, bf16[8,96,768]{2,1,0:T(8,128)(2,1)S(1)}, u32[]{:S(2)}, u32[]{:S(2)}) collective-permute-start(bf16[8,96,768]{2,1,0:T(8,128)(2,1)} %get-tuple-element.123), channel_id=1, source_target_pairs={{0,16},{1,3},{2,18},{3,1},{4,20},{5,7},{6,22},{7,5},{8,24},{9,11},... | collective-permute-start | bytes 3538952 | tf_op jit(solution)/shard_map/ppermute | solution.py:1049
  219.4 37.8 %collective-permute-start.56 = (bf16[4,96,768]{2,1,0:T(8,128)(2,1)S(1)}, bf16[4,96,768]{2,1,0:T(8,128)(2,1)S(1)}, u32[]{:S(2)}, u32[]{:S(2)}) collective-permute-start(bf16[4,96,768]{2,1,0:T(8,128)(2,1)S(1)} %get-tuple-element.139), channel_id=1, source_target_pairs={{0,2},{1,17},{2,0},{3,19},{4,6},{5,21},{6,4},{7,23},{8,10},{9,25},... | collective-permute-start | bytes 1769480 | tf_op jit(solution)/shard_map/ppermute | solution.py:1049
  236.7 27.0 %collective-permute-start.38 = (bf16[4,224,384]{2,1,0:T(8,128)(2,1)S(1)}, bf16[4,224,384]{2,1,0:T(8,128)(2,1)S(1)}, u32[]{:S(2)}, u32[]{:S(2)}) collective-permute-start(bf16[4,224,384]{2,1,0:T(8,128)(2,1)S(1)} %get-tuple-element.137), channel_id=1, source_target_pairs={{0,2},{1,17},{2,0},{3,19},{4,6},{5,21},{6,4},{7,23},{8,10},{9,25},... | collective-permute-start | bytes 2064392 | tf_op jit(solution)/shard_map/ppermute | solution.py:1049
  261.8 40.2 %collective-permute-start.58 = (bf16[96,768]{1,0:T(8,128)(2,1)S(1)}, bf16[96,768]{1,0:T(8,128)(2,1)S(1)}, u32[]{:S(2)}, u32[]{:S(2)}) collective-permute-start(bf16[96,768]{1,0:T(8,128)(2,1)S(1)} %get-tuple-element.147), channel_id=1, source_target_pairs={{0,8},{1,9},{2,10},{3,11},{4,12},{5,13},{6,14},{7,15},{8,0},{9,1},... | collective-permute-start | bytes 442376 | tf_op jit(solution)/shard_map/ppermute | solution.py:1049
  270.0 32.1 %collective-permute-start.59 = (bf16[96,768]{1,0:T(8,128)(2,1)S(1)}, bf16[96,768]{1,0:T(8,128)(2,1)S(1)}, u32[]{:S(2)}, u32[]{:S(2)}) collective-permute-start(bf16[96,768]{1,0:T(8,128)(2,1)S(1)} %get-tuple-element.146), channel_id=1, source_target_pairs={{0,12},{1,13},{2,14},{3,15},{4,0},{5,1},{6,2},{7,3},{8,4},{9,5},{1... | collective-permute-start | bytes 442376 | tf_op jit(solution)/shard_map/ppermute | solution.py:1049
  275.0 30.1 %collective-permute-start.50 = (bf16[96,768]{1,0:T(8,128)(2,1)S(1)}, bf16[96,768]{1,0:T(8,128)(2,1)S(1)}, u32[]{:S(2)}, u32[]{:S(2)}) collective-permute-start(bf16[96,768]{1,0:T(8,128)(2,1)S(1)} %get-tuple-element.152), channel_id=1, source_target_pairs={{0,4},{1,5},{2,6},{3,7},{4,8},{5,9},{6,10},{7,11},{8,12},{9,13},{1... | collective-permute-start | bytes 442376 | tf_op jit(solution)/shard_map/ppermute | solution.py:1049
  (93 other events, 946.4 us)
